TPU v7x, 32 devices: a whole 2x2x4 slice. The times are simulated.
32 devices in a mesh: lon: 8 (over z, y), lat: 4 (over x, core).
Axes of the slice: x: 2, y: 2, z: 4, core: 2. Of those that a mesh axis runs over, the one named last changes fastest.
Arguments:
- control: float32 [80, 128, 1024], P(None, 'lat', 'lon'), may hold values from -6 to 6
- diffusivity: float32 [128, 1024], P('lat', 'lon'), may hold values from 0.02 to 0.12
- land_mask: int32 [128, 1024], P('lat', 'lon'), may hold values 0 or 1
- innovations: float32 [4, 80, 1024], P('lat', None, 'lon'), may hold values from -6 to 6
- obs_sigma: float32 [4, 80, 1024], P('lat', None, 'lon'), may hold values from 0.5 to 2
- obs_row: int32 [4, 1024], P('lat', 'lon'), may hold values from 0 to 31
- obs_col: int32 [4, 1024], P('lat', 'lon'), may hold values from 0 to 127
- obs_frac: float32 [4, 2, 1024], P('lat', None, 'lon'), may hold values from 0 to 1
- obs_counts: int32 [4, 8], P('lat', 'lon'), may hold values from 32 to 128, as said below
Outputs:
- obs_gradient: float32 [80, 128, 1024], P(None, 'lat', 'lon')
- departures: float32 [4, 80, 1024], P('lat', None, 'lon')
Inputs may be any that keep to these rules, and one draw needn't show every extreme that they name: `obs_counts`: every tile holds between 32 and 128 live profiles in its first slots; some tile holds exactly 128.
All inputs are finite; a program needn't handle non-finite values. No bound on the sum of `land_mask` on one device may be relied on, other than what follows from the above.
Results may differ from a plain program's by a relative error of at most 0.00002.
Values sent between devices are 32-bit elements; how exact they have to be, the bound alone decides.
A program may use at most 64 MiB of HBM per device.

v0:
```python
import jax
import jax.numpy as jnp
from jax import lax
from jax.sharding import PartitionSpec as P


def with_halo(block, sides, width, periodic):
    for axis, dim in sides:
        count = lax.axis_size(axis)
        forward = [(i, i + 1) for i in range(count - 1)]
        if periodic:
            forward.append((count - 1, 0))
        backward = [(target, source) for source, target in forward]
        low = lax.ppermute(
            lax.slice_in_dim(block, block.shape[dim] - width, None, axis=dim), axis, forward
        )
        high = lax.ppermute(lax.slice_in_dim(block, 0, width, axis=dim), axis, backward)
        block = jnp.concatenate([low, block, high], axis=dim)
    return block


def shifted(block, axis, distance):
    devices = range(lax.axis_size(axis))
    route = [(i - distance, i) for i in devices if i - distance in devices]
    return lax.ppermute(block, axis, route)


def passed_along(value, axis, steps):
    count = lax.axis_size(axis)
    pairs = [(source, (source + steps) % count) for source in range(count)]
    return lax.ppermute(value, axis, pairs)


def window(array, offset_y, offset_x):
    return array[
        ...,
        1 + offset_y : array.shape[-2] - 1 + offset_y,
        1 + offset_x : array.shape[-1] - 1 + offset_x,
    ]


def diffuse(padded, kappa_pad, mask_pad):
    center = window(padded, 0, 0)
    kappa_mid = window(kappa_pad, 0, 0)
    mask_mid = window(mask_pad, 0, 0)
    result = center
    for offset_y, offset_x in ((0, 1), (0, -1), (1, 0), (-1, 0)):
        weight = (
            0.5
            * (kappa_mid + window(kappa_pad, offset_y, offset_x))
            * mask_mid
            * window(mask_pad, offset_y, offset_x)
        )
        result = result + weight * (window(padded, offset_y, offset_x) - center)
    return result


def pad_tile(field, width):
    lon_padded = with_halo(field, (("lon", 2),), width, True)
    return with_halo(lon_padded, (("lat", 1),), width, False)


def on_device(
    control, diffusivity, land_mask, innovations, obs_sigma, obs_row, obs_col, obs_frac, obs_counts
):
    depth = 1
    coeff = jnp.stack([diffusivity, land_mask.astype(jnp.float32)])
    coeff_pad = pad_tile(coeff, depth)

    def smooth(field):
        for repeat in range(2):
            field = diffuse(pad_tile(field, 1), coeff_pad[0], coeff_pad[1])
        return field

    padded = pad_tile(smooth(control), 1)
    channels = padded.shape[0]
    cols_pad = padded.shape[2]
    flat = padded.reshape(channels, -1)
    base = (obs_row[0] + 1) * cols_pad + obs_col[0] + 1
    offsets = jnp.stack([base, base + 1, base + cols_pad, base + cols_pad + 1])
    frac_y = obs_frac[0, 0]
    frac_x = obs_frac[0, 1]
    weights = jnp.stack(
        [
            (1.0 - frac_y) * (1.0 - frac_x),
            (1.0 - frac_y) * frac_x,
            frac_y * (1.0 - frac_x),
            frac_y * frac_x,
        ]
    )
    sample = jnp.sum(weights[None] * flat[:, offsets], axis=1)
    slots = jnp.arange(obs_row.shape[1], dtype=jnp.int32)
    valid = (slots < obs_counts[0, 0]).astype(jnp.float32)
    departure = valid * (sample - innovations[0])
    weighted = departure / (obs_sigma[0] * obs_sigma[0])
    spread = (weights[None] * weighted[:, None, :]).reshape(channels, -1)
    adjoint = jnp.zeros_like(flat).at[:, offsets.reshape(-1)].add(spread).reshape(padded.shape)
    north = shifted(adjoint[:, -1, :], "lat", 1)
    adjoint = adjoint.at[:, 1, :].add(north)
    east = passed_along(adjoint[:, 1:-1, -1], "lon", 1)
    inner = adjoint[:, 1:-1, 1:-1].at[:, :, 0].add(east)
    return (smooth(inner), departure[None])


def solution(mesh):
    in_specs = (
        P(None, "lat", "lon"),
        P("lat", "lon"),
        P("lat", "lon"),
        P("lat", None, "lon"),
        P("lat", None, "lon"),
        P("lat", "lon"),
        P("lat", "lon"),
        P("lat", None, "lon"),
        P("lat", "lon"),
    )
    out_specs = (P(None, "lat", "lon"), P("lat", None, "lon"))
    return jax.shard_map(
        on_device, mesh=mesh, in_specs=in_specs, out_specs=out_specs, check_vma=False
    )
```

profile of v0, /device:TPU:1, one launch (start us, length us, event | category | flops | bytes accessed | tf_op | source)
XLA Modules:
  0.0 128.1 jit_solution(2119263630700060406)
XLA Ops:
  2.3 2.1 %collective-permute-start = (f32[2,32,1]{2,1,0:T(8,128)S(1)}, f32[2,32,1]{2,1,0:T(8,128)S(1)}, u32[]{:S(2)}, u32[]{:S(2)}) collective-permute-start(f32[2,32,1]{2,1,0:T(8,128)S(1)} %get-tuple-element.60), channel_id=1, source_target_pairs={{0,4},{4,8},{8,12},{12,16},{16,20},{20,24},{24,28},{28,0},{1,5},{5... | collective-permute-start | bytes 776 | tf_op jit(solution)/shard_map/ppermute | solution.py:14
  4.3 3.1 %collective-permute-start.1 = (f32[2,32,1]{2,1,0:T(8,128)S(1)}, f32[2,32,1]{2,1,0:T(8,128)S(1)}, u32[]{:S(2)}, u32[]{:S(2)}) collective-permute-start(f32[2,32,1]{2,1,0:T(8,128)S(1)} %get-tuple-element.61), channel_id=1, source_target_pairs={{4,0},{8,4},{12,8},{16,12},{20,16},{24,20},{28,24},{0,28},{5,1},{9... | collective-permute-start | bytes 776 | tf_op jit(solution)/shard_map/ppermute | solution.py:17
  9.4 4.1 %collective-permute-start.4 = (f32[80,32,1]{0,2,1:T(1,128)S(1)}, f32[80,32,1]{0,2,1:T(1,128)S(1)}, u32[]{:S(2)}, u32[]{:S(2)}) collective-permute-start(f32[80,32,1]{0,2,1:T(1,128)S(1)} %get-tuple-element.51), channel_id=1, source_target_pairs={{4,0},{8,4},{12,8},{16,12},{20,16},{24,20},{28,24},{0,28},{5,1},{9... | collective-permute-start | bytes 30728 | tf_op jit(solution)/shard_map/ppermute | solution.py:17
  13.7 4.6 %collective-permute-start.2 = (f32[2,1,130]{2,1,0:T(1,128)S(1)}, f32[2,1,130]{2,1,0:T(1,128)S(1)}, u32[]{:S(2)}, u32[]{:S(2)}) collective-permute-start(f32[2,1,130]{2,1,0:T(1,128)S(1)} %get-tuple-element.52), channel_id=1, source_target_pairs={{0,1},{1,2},{2,3},{4,5},{5,6},{6,7},{8,9},{9,10},{10,11},{12,13},{... | collective-permute-start | bytes 3128 | tf_op jit(solution)/shard_map/ppermute | solution.py:14
  20.3 2.9 %collective-permute-done.3 = f32[2,1,130]{2,1,0:T(1,128)S(1)} collective-permute-done((f32[2,1,130]{2,1,0:T(1,128)S(1)}, f32[2,1,130]{2,1,0:T(1,128)S(1)}, u32[]{:S(2)}, u32[]{:S(2)}) %collective-permute-start.3) | collective-permute-done | bytes 1072 | tf_op jit(solution)/shard_map/ppermute | solution.py:17
  25.3 3.6 %collective-permute-start.7 = (f32[80,1,130]{0,2,1:T(8,128)S(1)}, f32[80,1,130]{0,2,1:T(8,128)S(1)}, u32[]{:S(2)}, u32[]{:S(2)}) collective-permute-start(f32[80,1,130]{0,2,1:T(8,128)S(1)} %get-tuple-element.43), channel_id=1, source_target_pairs={{0,1},{1,2},{2,3},{4,5},{5,6},{6,7},{8,9},{9,10},{10,11},{12,13},{... | collective-permute-start | bytes 124808 | tf_op jit(solution)/shard_map/ppermute | solution.py:14
  30.3 3.4 %fusion.38 = f32[80,32,128]{0,2,1:T(8,128)S(1)} fusion(f32[80,32,128]{0,2,1:T(8,128)S(1)} %copy.50, f32[80,1,130]{0,2,1:T(8,128)S(1)} %collective-permute-done.7, f32[80,32,1]{0,2,1:T(1,128)S(1)} %collective-permute-done.4, f32[80,32,1]{0,2,1:T(1,128)S(1)} %collective-permute-done.5, f32[80,1,130]{0,2,1:T(8,128)S(1)} %collective-permute-done.6, ...), kind=kLoop, calls=%fused_computation.66 | loop fusion | flops 6553600 | bytes 2790656 | tf_op jit(solution)/shard_map/add | solution.py:54
  33.9 4.1 %collective-permute-start.8 = (f32[80,32,1]{0,2,1:T(1,128)S(1)}, f32[80,32,1]{0,2,1:T(1,128)S(1)}, u32[]{:S(2)}, u32[]{:S(2)}) collective-permute-start(f32[80,32,1]{0,2,1:T(1,128)S(1)} %get-tuple-element.49), channel_id=1, source_target_pairs={{4,0},{8,4},{12,8},{16,12},{20,16},{24,20},{28,24},{0,28},{5,1},{9... | collective-permute-start | bytes 30728 | tf_op jit(solution)/shard_map/ppermute | solution.py:17
  41.1 5.4 %collective-permute-start.11 = (f32[80,1,130]{0,2,1:T(8,128)S(1)}, f32[80,1,130]{0,2,1:T(8,128)S(1)}, u32[]{:S(2)}, u32[]{:S(2)}) collective-permute-start(f32[80,1,130]{0,2,1:T(8,128)S(1)} %get-tuple-element.41), channel_id=1, source_target_pairs={{0,1},{1,2},{2,3},{4,5},{5,6},{6,7},{8,9},{9,10},{10,11},{12,13},{... | collective-permute-start | bytes 124808 | tf_op jit(solution)/shard_map/ppermute | solution.py:14
  47.9 3.5 %fusion.26 = f32[80,32,128]{0,2,1:T(8,128)S(1)} fusion(f32[80,32,128]{0,2,1:T(8,128)S(1)} %fusion.38, f32[80,1,130]{0,2,1:T(8,128)S(1)} %collective-permute-done.11, f32[80,32,1]{0,2,1:T(1,128)S(1)} %collective-permute-done.8, f32[80,32,1]{0,2,1:T(1,128)S(1)} %collective-permute-done.9, f32[80,1,130]{0,2,1:T(8,128)S(1)} %collective-permute-done.10, ...), kind=kLoop, calls=%fused_computation.46 | loop fusion | flops 6553600 | bytes 2790656 | tf_op jit(solution)/shard_map/add | solution.py:54
  51.5 4.5 %collective-permute-start.13 = (f32[80,32,1]{0,2,1:T(1,128)S(1)}, f32[80,32,1]{0,2,1:T(1,128)S(1)}, u32[]{:S(2)}, u32[]{:S(2)}) collective-permute-start(f32[80,32,1]{0,2,1:T(1,128)S(1)} %get-tuple-element.47), channel_id=1, source_target_pairs={{4,0},{8,4},{12,8},{16,12},{20,16},{24,20},{28,24},{0,28},{5,1},{9... | collective-permute-start | bytes 30728 | tf_op jit(solution)/shard_map/ppermute | solution.py:17
  57.0 5.1 %collective-permute-start.14 = (f32[80,1,130]{0,2,1:T(8,128)S(1)}, f32[80,1,130]{0,2,1:T(8,128)S(1)}, u32[]{:S(2)}, u32[]{:S(2)}) collective-permute-start(f32[80,1,130]{0,2,1:T(8,128)S(1)} %get-tuple-element.38), channel_id=1, source_target_pairs={{0,1},{1,2},{2,3},{4,5},{5,6},{6,7},{8,9},{9,10},{10,11},{12,13},{... | collective-permute-start | bytes 124808 | tf_op jit(solution)/shard_map/ppermute | solution.py:14
  64.1 3.7 %collective-permute-done.15 = f32[80,1,130]{0,2,1:T(8,128)S(1)} collective-permute-done((f32[80,1,130]{0,2,1:T(8,128)S(1)}, f32[80,1,130]{0,2,1:T(8,128)S(1)}, u32[]{:S(2)}, u32[]{:S(2)}) %collective-permute-start.15) | collective-permute-done | bytes 41632 | tf_op jit(solution)/shard_map/ppermute | solution.py:17
  69.7 2.7 %gather_fusion = f32[512,80]{1,0:T(8,128)S(1)} fusion(f32[80,4420]{0,1:T(8,128)} %reshape.376, s32[1024]{0:T(1024)S(1)} %pad_clamp_fusion), kind=kCustom, calls=%fused_computation | custom fusion | bytes 329728 | tf_op jit(solution)/shard_map/gather | solution.py:91
  72.9 3.8 %scatter_custom_fusion = f32[80,4420]{0,1:T(8,128)} fusion(s32[512]{0:T(512)S(1)} %bitcast.79, f32[]{:T(128)} %constant.66.clone.1, f32[80,512]{0,1:T(8,128)S(1)} %bitcast_multiply_fusion), kind=kCustom, calls=%fused_computation.83 | custom fusion | flops 40960 | bytes 1676548 | tf_op jit(solution)/shard_map/scatter-add | solution.py:97
  76.6 2.3 %reshape.377 = f32[80,34,130]{0,2,1:T(8,128)S(1)} reshape(f32[80,4420]{0,1:T(8,128)} %scatter_custom_fusion) | data formatting | bytes 2828800 | tf_op jit(solution)/shard_map/reshape | solution.py:97
  85.6 3.7 %collective-permute-done.17 = f32[80,32]{0,1:T(8,128)S(1)} collective-permute-done((f32[80,32]{0,1:T(8,128)S(1)}, f32[80,32]{0,1:T(8,128)S(1)}, u32[]{:S(2)}, u32[]{:S(2)}) %collective-permute-start.17) | collective-permute-done | bytes 10272 | tf_op jit(solution)/shard_map/ppermute | solution.py:31
  90.4 4.1 %collective-permute-start.18 = (f32[80,32,1]{0,2,1:T(1,128)S(1)}, f32[80,32,1]{0,2,1:T(1,128)S(1)}, u32[]{:S(2)}, u32[]{:S(2)}) collective-permute-start(f32[80,32,1]{0,2,1:T(1,128)S(1)} %slice_add_fusion.1), channel_id=1, source_target_pairs={{4,0},{8,4},{12,8},{16,12},{20,16},{24,20},{28,24},{0,28},{5,1},{9... | collective-permute-start | bytes 30728 | tf_op jit(solution)/shard_map/ppermute | solution.py:17
  95.7 4.0 %collective-permute-start.20 = (f32[80,1,130]{0,2,1:T(8,128)S(1)}, f32[80,1,130]{0,2,1:T(8,128)S(1)}, u32[]{:S(2)}, u32[]{:S(2)}) collective-permute-start(f32[80,1,130]{0,2,1:T(8,128)S(1)} %get-tuple-element.36), channel_id=1, source_target_pairs={{1,0},{2,1},{3,2},{5,4},{6,5},{7,6},{9,8},{10,9},{11,10},{13,12},{... | collective-permute-start | bytes 124808 | tf_op jit(solution)/shard_map/ppermute | solution.py:17
  99.7 4.2 %collective-permute-start.21 = (f32[80,1,130]{0,2,1:T(8,128)S(1)}, f32[80,1,130]{0,2,1:T(8,128)S(1)}, u32[]{:S(2)}, u32[]{:S(2)}) collective-permute-start(f32[80,1,130]{0,2,1:T(8,128)S(1)} %get-tuple-element.37), channel_id=1, source_target_pairs={{0,1},{1,2},{2,3},{4,5},{5,6},{6,7},{8,9},{9,10},{10,11},{12,13},{... | collective-permute-start | bytes 124808 | tf_op jit(solution)/shard_map/ppermute | solution.py:14
  105.3 3.4 %fusion.14 = f32[80,32,128]{0,2,1:T(8,128)S(1)} fusion(f32[80,32,128]{0,2,1:T(8,128)S(1)} %scatter-add.19, f32[80,1,130]{0,2,1:T(8,128)S(1)} %collective-permute-done.21, f32[80,32,1]{0,2,1:T(1,128)S(1)} %collective-permute-done.18, f32[80,32,1]{0,2,1:T(1,128)S(1)} %collective-permute-done.19, f32[80,1,130]{0,2,1:T(8,128)S(1)} %collective-permute-done.20, ...), kind=kLoop, calls=%fused_computation.26 | loop fusion | flops 6553600 | bytes 2790656 | tf_op jit(solution)/shard_map/add | solution.py:54
  108.8 4.5 %collective-permute-start.22 = (f32[80,32,1]{0,2,1:T(1,128)S(1)}, f32[80,32,1]{0,2,1:T(1,128)S(1)}, u32[]{:S(2)}, u32[]{:S(2)}) collective-permute-start(f32[80,32,1]{0,2,1:T(1,128)S(1)} %get-tuple-element.45), channel_id=1, source_target_pairs={{4,0},{8,4},{12,8},{16,12},{20,16},{24,20},{28,24},{0,28},{5,1},{9... | collective-permute-start | bytes 30728 | tf_op jit(solution)/shard_map/ppermute | solution.py:17
  116.4 5.1 %collective-permute-start.25 = (f32[80,1,130]{0,2,1:T(8,128)S(1)}, f32[80,1,130]{0,2,1:T(8,128)S(1)}, u32[]{:S(2)}, u32[]{:S(2)}) collective-permute-start(f32[80,1,130]{0,2,1:T(8,128)S(1)} %get-tuple-element.35), channel_id=1, source_target_pairs={{0,1},{1,2},{2,3},{4,5},{5,6},{6,7},{8,9},{9,10},{10,11},{12,13},{... | collective-permute-start | bytes 124808 | tf_op jit(solution)/shard_map/ppermute | solution.py:14
  122.9 3.5 %fusion.2 = f32[80,32,128]{0,2,1:T(8,128)S(1)} fusion(f32[80,32,128]{0,2,1:T(8,128)S(1)} %fusion.14, f32[80,1,130]{0,2,1:T(8,128)S(1)} %collective-permute-done.25, f32[80,32,1]{0,2,1:T(1,128)S(1)} %collective-permute-done.22, f32[80,32,1]{0,2,1:T(1,128)S(1)} %collective-permute-done.23, f32[80,1,130]{0,2,1:T(8,128)S(1)} %collective-permute-done.24, ...), kind=kLoop, calls=%fused_computation.6 | loop fusion | flops 6553600 | bytes 2790656 | tf_op jit(solution)/shard_map/add | solution.py:54
  (90 shorter events, 34.5 us)
Async XLA Ops:
  2.3 11.3 %collective-permute-start = (f32[2,32,1]{2,1,0:T(8,128)S(1)}, f32[2,32,1]{2,1,0:T(8,128)S(1)}, u32[]{:S(2)}, u32[]{:S(2)}) collective-permute-start(f32[2,32,1]{2,1,0:T(8,128)S(1)} %get-tuple-element.60), channel_id=1, source_target_pairs={{0,4},{4,8},{8,12},{12,16},{16,20},{20,24},{24,28},{28,0},{1,5},{5... | collective-permute-start | bytes 776 | tf_op jit(solution)/shard_map/ppermute | solution.py:14
  4.3 9.2 %collective-permute-start.1 = (f32[2,32,1]{2,1,0:T(8,128)S(1)}, f32[2,32,1]{2,1,0:T(8,128)S(1)}, u32[]{:S(2)}, u32[]{:S(2)}) collective-permute-start(f32[2,32,1]{2,1,0:T(8,128)S(1)} %get-tuple-element.61), channel_id=1, source_target_pairs={{4,0},{8,4},{12,8},{16,12},{20,16},{24,20},{28,24},{0,28},{5,1},{9... | collective-permute-start | bytes 776 | tf_op jit(solution)/shard_map/ppermute | solution.py:17
  9.3 14.1 %collective-permute-start.5 = (f32[80,32,1]{0,2,1:T(1,128)S(1)}, f32[80,32,1]{0,2,1:T(1,128)S(1)}, u32[]{:S(2)}, u32[]{:S(2)}) collective-permute-start(f32[80,32,1]{0,2,1:T(1,128)S(1)} %get-tuple-element.50), channel_id=1, source_target_pairs={{0,4},{4,8},{8,12},{12,16},{16,20},{20,24},{24,28},{28,0},{1,5},{5... | collective-permute-start | bytes 30728 | tf_op jit(solution)/shard_map/ppermute | solution.py:14
  9.4 14.0 %collective-permute-start.4 = (f32[80,32,1]{0,2,1:T(1,128)S(1)}, f32[80,32,1]{0,2,1:T(1,128)S(1)}, u32[]{:S(2)}, u32[]{:S(2)}) collective-permute-start(f32[80,32,1]{0,2,1:T(1,128)S(1)} %get-tuple-element.51), channel_id=1, source_target_pairs={{4,0},{8,4},{12,8},{16,12},{20,16},{24,20},{28,24},{0,28},{5,1},{9... | collective-permute-start | bytes 30728 | tf_op jit(solution)/shard_map/ppermute | solution.py:17
  13.7 6.6 %collective-permute-start.2 = (f32[2,1,130]{2,1,0:T(1,128)S(1)}, f32[2,1,130]{2,1,0:T(1,128)S(1)}, u32[]{:S(2)}, u32[]{:S(2)}) collective-permute-start(f32[2,1,130]{2,1,0:T(1,128)S(1)} %get-tuple-element.52), channel_id=1, source_target_pairs={{0,1},{1,2},{2,3},{4,5},{5,6},{6,7},{8,9},{9,10},{10,11},{12,13},{... | collective-permute-start | bytes 3128 | tf_op jit(solution)/shard_map/ppermute | solution.py:14
  23.4 5.7 %collective-permute-start.6 = (f32[80,1,130]{0,2,1:T(8,128)S(1)}, f32[80,1,130]{0,2,1:T(8,128)S(1)}, u32[]{:S(2)}, u32[]{:S(2)}) collective-permute-start(f32[80,1,130]{0,2,1:T(8,128)S(1)} %get-tuple-element.42), channel_id=1, source_target_pairs={{1,0},{2,1},{3,2},{5,4},{6,5},{7,6},{9,8},{10,9},{11,10},{13,12},{... | collective-permute-start | bytes 124808 | tf_op jit(solution)/shard_map/ppermute | solution.py:17
  25.3 5.0 %collective-permute-start.7 = (f32[80,1,130]{0,2,1:T(8,128)S(1)}, f32[80,1,130]{0,2,1:T(8,128)S(1)}, u32[]{:S(2)}, u32[]{:S(2)}) collective-permute-start(f32[80,1,130]{0,2,1:T(8,128)S(1)} %get-tuple-element.43), channel_id=1, source_target_pairs={{0,1},{1,2},{2,3},{4,5},{5,6},{6,7},{8,9},{9,10},{10,11},{12,13},{... | collective-permute-start | bytes 124808 | tf_op jit(solution)/shard_map/ppermute | solution.py:14
  33.8 5.3 %collective-permute-start.9 = (f32[80,32,1]{0,2,1:T(1,128)S(1)}, f32[80,32,1]{0,2,1:T(1,128)S(1)}, u32[]{:S(2)}, u32[]{:S(2)}) collective-permute-start(f32[80,32,1]{0,2,1:T(1,128)S(1)} %get-tuple-element.48), channel_id=1, source_target_pairs={{0,4},{4,8},{8,12},{12,16},{16,20},{20,24},{24,28},{28,0},{1,5},{5... | collective-permute-start | bytes 30728 | tf_op jit(solution)/shard_map/ppermute | solution.py:14
  33.9 5.3 %collective-permute-start.8 = (f32[80,32,1]{0,2,1:T(1,128)S(1)}, f32[80,32,1]{0,2,1:T(1,128)S(1)}, u32[]{:S(2)}, u32[]{:S(2)}) collective-permute-start(f32[80,32,1]{0,2,1:T(1,128)S(1)} %get-tuple-element.49), channel_id=1, source_target_pairs={{4,0},{8,4},{12,8},{16,12},{20,16},{24,20},{28,24},{0,28},{5,1},{9... | collective-permute-start | bytes 30728 | tf_op jit(solution)/shard_map/ppermute | solution.py:17
  39.2 7.4 %collective-permute-start.10 = (f32[80,1,130]{0,2,1:T(8,128)S(1)}, f32[80,1,130]{0,2,1:T(8,128)S(1)}, u32[]{:S(2)}, u32[]{:S(2)}) collective-permute-start(f32[80,1,130]{0,2,1:T(8,128)S(1)} %get-tuple-element.40), channel_id=1, source_target_pairs={{1,0},{2,1},{3,2},{5,4},{6,5},{7,6},{9,8},{10,9},{11,10},{13,12},{... | collective-permute-start | bytes 124808 | tf_op jit(solution)/shard_map/ppermute | solution.py:17
  41.1 6.8 %collective-permute-start.11 = (f32[80,1,130]{0,2,1:T(8,128)S(1)}, f32[80,1,130]{0,2,1:T(8,128)S(1)}, u32[]{:S(2)}, u32[]{:S(2)}) collective-permute-start(f32[80,1,130]{0,2,1:T(8,128)S(1)} %get-tuple-element.41), channel_id=1, source_target_pairs={{0,1},{1,2},{2,3},{4,5},{5,6},{6,7},{8,9},{9,10},{10,11},{12,13},{... | collective-permute-start | bytes 124808 | tf_op jit(solution)/shard_map/ppermute | solution.py:14
  51.4 5.6 %collective-permute-start.12 = (f32[80,32,1]{0,2,1:T(1,128)S(1)}, f32[80,32,1]{0,2,1:T(1,128)S(1)}, u32[]{:S(2)}, u32[]{:S(2)}) collective-permute-start(f32[80,32,1]{0,2,1:T(1,128)S(1)} %get-tuple-element.46), channel_id=1, source_target_pairs={{0,4},{4,8},{8,12},{12,16},{16,20},{20,24},{24,28},{28,0},{1,5},{5... | collective-permute-start | bytes 30728 | tf_op jit(solution)/shard_map/ppermute | solution.py:14
  51.5 5.6 %collective-permute-start.13 = (f32[80,32,1]{0,2,1:T(1,128)S(1)}, f32[80,32,1]{0,2,1:T(1,128)S(1)}, u32[]{:S(2)}, u32[]{:S(2)}) collective-permute-start(f32[80,32,1]{0,2,1:T(1,128)S(1)} %get-tuple-element.47), channel_id=1, source_target_pairs={{4,0},{8,4},{12,8},{16,12},{20,16},{24,20},{28,24},{0,28},{5,1},{9... | collective-permute-start | bytes 30728 | tf_op jit(solution)/shard_map/ppermute | solution.py:17
  57.0 7.1 %collective-permute-start.14 = (f32[80,1,130]{0,2,1:T(8,128)S(1)}, f32[80,1,130]{0,2,1:T(8,128)S(1)}, u32[]{:S(2)}, u32[]{:S(2)}) collective-permute-start(f32[80,1,130]{0,2,1:T(8,128)S(1)} %get-tuple-element.38), channel_id=1, source_target_pairs={{0,1},{1,2},{2,3},{4,5},{5,6},{6,7},{8,9},{9,10},{10,11},{12,13},{... | collective-permute-start | bytes 124808 | tf_op jit(solution)/shard_map/ppermute | solution.py:14
  62.2 5.6 %collective-permute-start.15 = (f32[80,1,130]{0,2,1:T(8,128)S(1)}, f32[80,1,130]{0,2,1:T(8,128)S(1)}, u32[]{:S(2)}, u32[]{:S(2)}) collective-permute-start(f32[80,1,130]{0,2,1:T(8,128)S(1)} %get-tuple-element.39), channel_id=1, source_target_pairs={{1,0},{2,1},{3,2},{5,4},{6,5},{7,6},{9,8},{10,9},{11,10},{13,12},{... | collective-permute-start | bytes 124808 | tf_op jit(solution)/shard_map/ppermute | solution.py:17
  83.7 5.6 %collective-permute-start.17 = (f32[80,32]{0,1:T(8,128)S(1)}, f32[80,32]{0,1:T(8,128)S(1)}, u32[]{:S(2)}, u32[]{:S(2)}) collective-permute-start(f32[80,32]{0,1:T(8,128)S(1)} %bitcast.76), channel_id=1, source_target_pairs={{0,4},{4,8},{8,12},{12,16},{16,20},{20,24},{24,28},{28,0},{1,5},{5... | collective-permute-start | bytes 30728 | tf_op jit(solution)/shard_map/ppermute | solution.py:31
  90.4 5.3 %collective-permute-start.19 = (f32[80,32,1]{0,2,1:T(1,128)S(1)}, f32[80,32,1]{0,2,1:T(1,128)S(1)}, u32[]{:S(2)}, u32[]{:S(2)}) collective-permute-start(f32[80,32,1]{0,2,1:T(1,128)S(1)} %slice.351), channel_id=1, source_target_pairs={{0,4},{4,8},{8,12},{12,16},{16,20},{20,24},{24,28},{28,0},{1,5},{5... | collective-permute-start | bytes 30728 | tf_op jit(solution)/shard_map/ppermute | solution.py:14
  90.4 5.3 %collective-permute-start.18 = (f32[80,32,1]{0,2,1:T(1,128)S(1)}, f32[80,32,1]{0,2,1:T(1,128)S(1)}, u32[]{:S(2)}, u32[]{:S(2)}) collective-permute-start(f32[80,32,1]{0,2,1:T(1,128)S(1)} %slice_add_fusion.1), channel_id=1, source_target_pairs={{4,0},{8,4},{12,8},{16,12},{20,16},{24,20},{28,24},{0,28},{5,1},{9... | collective-permute-start | bytes 30728 | tf_op jit(solution)/shard_map/ppermute | solution.py:17
  95.7 8.3 %collective-permute-start.20 = (f32[80,1,130]{0,2,1:T(8,128)S(1)}, f32[80,1,130]{0,2,1:T(8,128)S(1)}, u32[]{:S(2)}, u32[]{:S(2)}) collective-permute-start(f32[80,1,130]{0,2,1:T(8,128)S(1)} %get-tuple-element.36), channel_id=1, source_target_pairs={{1,0},{2,1},{3,2},{5,4},{6,5},{7,6},{9,8},{10,9},{11,10},{13,12},{... | collective-permute-start | bytes 124808 | tf_op jit(solution)/shard_map/ppermute | solution.py:17
  99.7 5.6 %collective-permute-start.21 = (f32[80,1,130]{0,2,1:T(8,128)S(1)}, f32[80,1,130]{0,2,1:T(8,128)S(1)}, u32[]{:S(2)}, u32[]{:S(2)}) collective-permute-start(f32[80,1,130]{0,2,1:T(8,128)S(1)} %get-tuple-element.37), channel_id=1, source_target_pairs={{0,1},{1,2},{2,3},{4,5},{5,6},{6,7},{8,9},{9,10},{10,11},{12,13},{... | collective-permute-start | bytes 124808 | tf_op jit(solution)/shard_map/ppermute | solution.py:14
  108.8 5.6 %collective-permute-start.23 = (f32[80,32,1]{0,2,1:T(1,128)S(1)}, f32[80,32,1]{0,2,1:T(1,128)S(1)}, u32[]{:S(2)}, u32[]{:S(2)}) collective-permute-start(f32[80,32,1]{0,2,1:T(1,128)S(1)} %get-tuple-element.44), channel_id=1, source_target_pairs={{0,4},{4,8},{8,12},{12,16},{16,20},{20,24},{24,28},{28,0},{1,5},{5... | collective-permute-start | bytes 30728 | tf_op jit(solution)/shard_map/ppermute | solution.py:14
  108.8 5.6 %collective-permute-start.22 = (f32[80,32,1]{0,2,1:T(1,128)S(1)}, f32[80,32,1]{0,2,1:T(1,128)S(1)}, u32[]{:S(2)}, u32[]{:S(2)}) collective-permute-start(f32[80,32,1]{0,2,1:T(1,128)S(1)} %get-tuple-element.45), channel_id=1, source_target_pairs={{4,0},{8,4},{12,8},{16,12},{20,16},{24,20},{28,24},{0,28},{5,1},{9... | collective-permute-start | bytes 30728 | tf_op jit(solution)/shard_map/ppermute | solution.py:17
  114.4 7.7 %collective-permute-start.24 = (f32[80,1,130]{0,2,1:T(8,128)S(1)}, f32[80,1,130]{0,2,1:T(8,128)S(1)}, u32[]{:S(2)}, u32[]{:S(2)}) collective-permute-start(f32[80,1,130]{0,2,1:T(8,128)S(1)} %get-tuple-element.34), channel_id=1, source_target_pairs={{1,0},{2,1},{3,2},{5,4},{6,5},{7,6},{9,8},{10,9},{11,10},{13,12},{... | collective-permute-start | bytes 124808 | tf_op jit(solution)/shard_map/ppermute | solution.py:17
  116.4 6.5 %collective-permute-start.25 = (f32[80,1,130]{0,2,1:T(8,128)S(1)}, f32[80,1,130]{0,2,1:T(8,128)S(1)}, u32[]{:S(2)}, u32[]{:S(2)}) collective-permute-start(f32[80,1,130]{0,2,1:T(8,128)S(1)} %get-tuple-element.35), channel_id=1, source_target_pairs={{0,1},{1,2},{2,3},{4,5},{5,6},{6,7},{8,9},{9,10},{10,11},{12,13},{... | collective-permute-start | bytes 124808 | tf_op jit(solution)/shard_map/ppermute | solution.py:14
  (9 other events, 76.9 us)
where the time goes:
time: 129 us; the launch traced here: 128 us
  starting transfers between devices  70.6 us (55%)
  other arithmetic  21.7 us (17%)
  waiting for transfers between devices  20.1 us (16%)
  local copies, waits for them, and re-layouts  13.8 us (11%)
  between operations  1.85 us (1%)
    ppermute x12, starting transfers between devices, with_halo(): lax.ppermute(lax.slice_in_dim(block, 0, width, axis=dim), axis, backward)  38.1 us
    ppermute x12, starting transfers between devices, with_halo(): lax.ppermute(lax.slice_in_dim(block, block.shape[dim] - width, None, axis...  30.6 us
    add x4, other arithmetic, diffuse(): result = result + weight * (window(padded, offset_y, offset_x) - center)  13.8 us
    ppermute x12, waiting for transfers between devices, with_halo(): lax.ppermute(lax.slice_in_dim(block, block.shape[dim] - width, None, axis...  8.26 us
    ppermute x12, waiting for transfers between devices, with_halo(): lax.ppermute(lax.slice_in_dim(block, 0, width, axis=dim), axis, backward)  6.73 us
    unnamed x16, local copies, waits for them, and re-layouts  5 us
    scatter-add x1, other arithmetic, on_device(): jnp.zeros_like(flat).at[:, offsets.reshape(-1)].add(spread)  3.75 us
    ppermute x1, waiting for transfers between devices, passed_along(): return lax.ppermute(value, axis, pairs)  3.74 us
  transfers between devices with their start and end apart: 26, of which 12 were waited for; matrix products, arithmetic and copies ran while one was open for 4% of the time, Pallas kernels for 0%

commit v1 on v0

v1 whole, which is shorter than its diff:
```python
import functools

import jax
import jax.numpy as jnp
from jax import lax
from jax.experimental import pallas as pl
from jax.experimental.pallas import tpu as pltpu
from jax.sharding import PartitionSpec as P

F32 = jnp.float32
BF16 = jnp.bfloat16
PACK = 16
SLOT = 8
EDGE = 4
MESH = pl.DeviceIdType.MESH


def kernel(
    levels,
    control, diffusivity, land_mask, innovations, sigma, obs_row, obs_col, frac, counts,
    gradient, departures,
    coeff, weights, strip_weights, hot_in, hot_out, work, adjoint,
    pack, rows_up, rows_dn, prow_up, prow_dn,
    pack_e, pack_w, got_up, got_dn, pgot_up, pgot_dn,
    bpack, brow_up, brow_dn, bprow_up, bprow_dn,
    bpack_e, bpack_w, bgot_up, bgot_dn, bpgot_up, bpgot_dn,
    send_sem, recv_sem, bsend_sem, brecv_sem,
):
    ty, tx = control.shape[1], control.shape[2]
    ext = ty + 8
    groups = levels // PACK
    lon, lat = lax.axis_index("lon"), lax.axis_index("lat")
    n_lon, n_lat = lax.axis_size("lon"), lax.axis_size("lat")
    east, west = lax.rem(lon + 1, n_lon), lax.rem(lon + n_lon - 1, n_lon)
    has_up, has_dn = lat < n_lat - 1, lat > 0
    columns = (lon, east, west)

    barrier = pltpu.get_barrier_semaphore()

    def greet(x, y):
        pl.semaphore_signal(barrier, inc=1, device_id={"lon": x, "lat": y}, device_id_type=MESH)

    greet(east, lat)
    greet(west, lat)

    @pl.when(has_up)
    def _():
        for x in columns:
            greet(x, lat + 1)

    @pl.when(has_dn)
    def _():
        for x in columns:
            greet(x, lat - 1)

    def copy(src, dst, sends, recvs, index, x, y):
        return pltpu.make_async_remote_copy(
            src_ref=src, dst_ref=dst, send_sem=sends.at[index], recv_sem=recvs.at[index],
            device_id={"lon": x, "lat": y}, device_id_type=MESH,
        )

    place = (0, 2, 1)

    lane = lax.broadcasted_iota(jnp.int32, (ext, tx), 1)
    slot = lax.rem(lane, SLOT)
    sub8 = lax.broadcasted_iota(jnp.int32, (8, tx), 0)

    coeff[0] = diffusivity[...]
    coeff[1] = land_mask[...].astype(F32)
    rows_up[0:levels] = control[:, ty - EDGE : ty, :]
    rows_dn[0:levels] = control[:, 0:EDGE, :]
    rows_up[levels : levels + 2] = coeff[:, ty - EDGE : ty, :]
    rows_dn[levels : levels + 2] = coeff[:, 0:EDGE, :]

    lane_t = lane[0:ty]

    def pack_group(g, carry):
        acc = jnp.zeros((ty, tx), F32)
        for p in range(PACK):
            x = control[g * PACK + p]
            acc = jnp.where(lane_t // SLOT == p, pltpu.roll(x, SLOT * p + 2, 1), acc)
        pack[g] = acc
        return carry

    lax.fori_loop(0, groups, pack_group, 0)
    for k in range(2):
        base = jnp.where(lane_t < SLOT, pltpu.roll(coeff[k], 2, 1), 0.0)
        width = SLOT
        while width < tx:
            base = base + pltpu.roll(base, width, 1)
            width *= 2
        pack[groups + k] = base
    prow_up[...] = pack[:, ty - EDGE : ty, :]
    prow_dn[...] = pack[:, 0:EDGE, :]

    @pl.when(jnp.logical_and(has_up, has_dn))
    def _():
        pl.semaphore_wait(barrier, 8)

    @pl.when(jnp.logical_not(jnp.logical_and(has_up, has_dn)))
    def _():
        pl.semaphore_wait(barrier, 5)

    side_copies = (
        copy(pack, pack_w, send_sem, recv_sem, 0, east, lat),
        copy(pack, pack_e, send_sem, recv_sem, 1, west, lat),
    )

    def up_copies():
        return [copy(rows_up, got_dn, send_sem, recv_sem, 2, lon, lat + 1)] + [
            copy(prow_up, pgot_dn.at[place[i]], send_sem, recv_sem, 4 + i, columns[i], lat + 1)
            for i in range(3)
        ]

    def dn_copies():
        return [copy(rows_dn, got_up, send_sem, recv_sem, 3, lon, lat - 1)] + [
            copy(prow_dn, pgot_up.at[place[i]], send_sem, recv_sem, 7 + i, columns[i], lat - 1)
            for i in range(3)
        ]

    for c in side_copies:
        c.start()

    @pl.when(has_up)
    def _():
        for c in up_copies():
            c.start()

    @pl.when(has_dn)
    def _():
        for c in dn_copies():
            c.start()

    col = obs_col[...]
    row = obs_row[...]
    cell = lax.broadcasted_iota(jnp.int32, (tx, tx), 0)
    kind = lax.rem(cell, SLOT)

    def hot(wanted):
        return jnp.concatenate(
            [jnp.where(col == wanted, 1.0, 0.0), jnp.where(col + 1 == wanted, 1.0, 0.0)], axis=1
        ).astype(BF16)

    main_hot = hot(cell)
    hot_in[0:tx] = main_hot
    hot_in[tx : 2 * tx] = hot(jnp.where(kind == 2, tx, -9))
    chosen = jnp.where(
        kind < 3, tx - 2 + kind, jnp.where(kind == 5, 0, jnp.where(kind == 6, 1, jnp.where(kind == 7, 0, -9)))
    )
    hot_out[0:tx] = main_hot
    hot_out[tx : 2 * tx] = hot(chosen)

    frac_y = frac[0, 0:1, :]
    frac_x = frac[0, 1:2, :]
    line = lax.broadcasted_iota(jnp.int32, (ext, tx), 0)
    row_weight = jnp.where(line == row, 1.0 - frac_y, 0.0) + jnp.where(line == row + 1, frac_y, 0.0)
    row_weight = jnp.where(jnp.logical_and(line == ty, lat == n_lat - 1), 0.0, row_weight)
    live = lax.broadcasted_iota(jnp.int32, (PACK, tx), 1) < counts[0, 0]

    for c in side_copies:
        c.wait()

    @pl.when(has_up)
    def _():
        for c in up_copies():
            c.wait_send()
        for c in dn_copies():
            c.wait_recv()

    @pl.when(has_dn)
    def _():
        for c in dn_copies():
            c.wait_send()
        for c in up_copies():
            c.wait_recv()

    @pl.when(jnp.logical_not(has_up))
    def _():
        got_up[...] = jnp.zeros_like(got_up)
        pgot_up[...] = jnp.zeros_like(pgot_up)

    @pl.when(jnp.logical_not(has_dn))
    def _():
        got_dn[...] = jnp.zeros_like(got_dn)
        pgot_dn[...] = jnp.zeros_like(pgot_dn)

    def strip_of(k):
        own = jnp.concatenate([pack[k], pgot_up[0, k], pgot_dn[0, k]], axis=0)
        e = jnp.concatenate([pack_e[k], pgot_up[1, k], pgot_dn[1, k]], axis=0)
        w = jnp.concatenate([pack_w[k], pgot_up[2, k], pgot_dn[2, k]], axis=0)
        far = jnp.where(slot == 7, pltpu.roll(own, 5, 1), pltpu.roll(w, 5, 1))
        return jnp.where(slot < 2, own, jnp.where(slot < 5, e, far))

    def edge_of(strip):
        return jnp.where(slot == 2, strip, pltpu.roll(strip, tx - 3, 1))

    def around(x, fill):
        left, right = pltpu.roll(x, 1, 1), pltpu.roll(x, tx - 1, 1)
        if fill is not None:
            left = jnp.where(lane == 0, fill, left)
            right = jnp.where(lane == tx - 1, fill, right)
        return left, right, pltpu.roll(x, 1, 0), pltpu.roll(x, ext - 1, 0)

    def fill_of(edge, p):
        return pltpu.roll(edge, (tx - 3 - SLOT * p) % tx, 1)

    def make_weights(dst, kappa, mask, kappas, masks):
        total = jnp.zeros_like(kappa)
        for i in range(4):
            w = 0.5 * (kappa + kappas[i]) * mask * masks[i]
            dst[i] = w
            total = total + w
        dst[4] = 1.0 - total

    kappa_strip, mask_strip = strip_of(groups), strip_of(groups + 1)
    make_weights(
        strip_weights, kappa_strip, mask_strip, around(kappa_strip, None), around(mask_strip, None)
    )
    kappa = jnp.concatenate([coeff[0], got_up[levels], got_dn[levels]], axis=0)
    mask = jnp.concatenate([coeff[1], got_up[levels + 1], got_dn[levels + 1]], axis=0)
    make_weights(
        weights, kappa, mask,
        around(kappa, fill_of(edge_of(kappa_strip), 0)),
        around(mask, fill_of(edge_of(mask_strip), 0)),
    )

    def diffuse(x, fill, w):
        near = around(x, fill)
        out = w[4] * x
        for i in range(4):
            out = out + w[i] * near[i]
        return out

    def parts(x):
        a = x.astype(BF16)
        rest = x - a.astype(F32)
        b = rest.astype(BF16)
        return a, b, (rest - b.astype(F32)).astype(BF16)

    def dot(x, y, dims):
        total = None
        for part in parts(x):
            one = lax.dot_general(part, y, (dims, ((), ())), preferred_element_type=F32)
            total = one if total is None else total + one
        return total

    def back_sides(g):
        return (
            copy(bpack.at[g], bpack_w.at[g], bsend_sem, brecv_sem, g * 10, east, lat),
            copy(bpack.at[g], bpack_e.at[g], bsend_sem, brecv_sem, g * 10 + 1, west, lat),
        )

    def back_up(g):
        mine = pl.ds(g * PACK, PACK)
        return [copy(brow_up.at[mine], bgot_dn.at[mine], bsend_sem, brecv_sem, g * 10 + 2, lon, lat + 1)] + [
            copy(bprow_up.at[g], bpgot_dn.at[place[i], g], bsend_sem, brecv_sem, g * 10 + 4 + i, columns[i], lat + 1)
            for i in range(3)
        ]

    def back_dn(g):
        mine = pl.ds(g * PACK, PACK)
        return [copy(brow_dn.at[mine], bgot_up.at[mine], bsend_sem, brecv_sem, g * 10 + 3, lon, lat - 1)] + [
            copy(bprow_dn.at[g], bpgot_up.at[place[i], g], bsend_sem, brecv_sem, g * 10 + 7 + i, columns[i], lat - 1)
            for i in range(3)
        ]

    def forward(g, carry):
        strip0 = strip_of(g)
        edge0 = edge_of(strip0)
        strip1 = diffuse(strip0, None, strip_weights)
        edge1 = edge_of(strip1)
        strip2 = diffuse(strip1, None, strip_weights)
        for p in range(PACK):
            level = g * PACK + p
            x = jnp.concatenate([control[level], got_up[level], got_dn[level]], axis=0)
            x = diffuse(x, fill_of(edge0, p), weights)
            x = diffuse(x, fill_of(edge1, p), weights)
            work[p, :, 0:tx] = x
            work[p, :, tx : 2 * tx] = jnp.where(lane // SLOT == p, strip2, 0.0)
        picked = dot(work[...].reshape(PACK * ext, 2 * tx), hot_in[...], ((1,), (0,)))
        mixed = picked[:, 0:tx] * (1.0 - frac_x) + picked[:, tx : 2 * tx] * frac_x
        sample = jnp.sum(mixed.reshape(PACK, ext, tx) * row_weight[None], axis=1)
        mine = pl.ds(g * PACK, PACK)
        departure = jnp.where(live, sample - innovations[0, mine, :], 0.0)
        departures[0, mine, :] = departure
        s = sigma[0, mine, :]
        weighted = departure / (s * s)
        spread = weighted[:, None, :] * row_weight[None]
        work[:, :, 0:tx] = spread * (1.0 - frac_x)[None]
        work[:, :, tx : 2 * tx] = spread * frac_x[None]
        field = dot(work[...].reshape(PACK * ext, 2 * tx), hot_out[...], ((1,), (1,)))
        adjoint[mine] = field[:, 0:tx].reshape(PACK, ext, tx)
        sides = field[:, tx : 2 * tx].reshape(PACK, ext, tx)
        acc = sides[0]
        for p in range(1, PACK):
            acc = jnp.where(lane // SLOT == p, sides[p], acc)
        bpack[g] = acc
        brow_up[mine] = adjoint[mine, ty - 3 : ty + 1, :]
        brow_dn[mine] = adjoint[mine, 0:EDGE, :]
        bprow_up[g] = bpack[g, ty - 3 : ty + 1, :]
        bprow_dn[g] = bpack[g, 0:EDGE, :]
        for c in back_sides(g):
            c.start()

        @pl.when(has_up)
        def _():
            for c in back_up(g):
                c.start()

        @pl.when(has_dn)
        def _():
            for c in back_dn(g):
                c.start()

        return carry

    lax.fori_loop(0, groups, forward, 0)

    @pl.when(jnp.logical_not(has_up))
    def _():
        bgot_up[...] = jnp.zeros_like(bgot_up)
        bpgot_up[...] = jnp.zeros_like(bpgot_up)

    @pl.when(jnp.logical_not(has_dn))
    def _():
        bgot_dn[...] = jnp.zeros_like(bgot_dn)
        bpgot_dn[...] = jnp.zeros_like(bpgot_dn)

    def with_rows(x, above, below):
        zero = jnp.zeros((EDGE, tx), F32)
        low = pltpu.roll(jnp.concatenate([zero, below], axis=0), 1, 0)
        first = x[0:8] + jnp.where(sub8 == 0, low, 0.0)
        last = x[ty:ext] + jnp.where(sub8 > 4, low, jnp.concatenate([above, zero], axis=0))
        return jnp.concatenate([first, x[8:ty], last], axis=0)

    def backward(g, carry):
        for c in back_sides(g):
            c.wait()

        @pl.when(has_up)
        def _():
            for c in back_up(g):
                c.wait_send()
            for c in back_dn(g):
                c.wait_recv()

        @pl.when(has_dn)
        def _():
            for c in back_dn(g):
                c.wait_send()
            for c in back_up(g):
                c.wait_recv()

        own = with_rows(bpack[g], bpgot_up[0, g], bpgot_dn[0, g])
        e = with_rows(bpack_e[g], bpgot_up[1, g], bpgot_dn[1, g])
        w = with_rows(bpack_w[g], bpgot_up[2, g], bpgot_dn[2, g])
        from_e = pltpu.roll(e, tx - 3, 1)
        from_w = pltpu.roll(w, 5, 1)
        strip = jnp.where(jnp.logical_or(slot < 3, slot == 7), own, 0.0)
        strip = strip + jnp.where(jnp.logical_or(slot == 2, slot == 3), from_e, 0.0)
        strip = strip + jnp.where(slot > 4, from_w, 0.0)
        first_col = jnp.where(slot == 7, from_w, 0.0)
        edge0 = edge_of(strip)
        edge1 = edge_of(diffuse(strip, None, strip_weights))
        for p in range(PACK):
            level = g * PACK + p
            x = with_rows(adjoint[level], bgot_up[level], bgot_dn[level])
            extra = pltpu.roll(first_col, (tx - 7 - SLOT * p) % tx, 1)
            x = x + jnp.where(lane == 0, extra, 0.0)
            x = diffuse(x, fill_of(edge0, p), weights)
            x = diffuse(x, fill_of(edge1, p), weights)
            gradient[level] = x[0:ty]
        return carry

    lax.fori_loop(0, groups, backward, 0)


def on_device(
    control, diffusivity, land_mask, innovations, obs_sigma, obs_row, obs_col, obs_frac, obs_counts
):
    levels, ty, tx = control.shape
    ext = ty + 8
    groups = levels // PACK
    vmem = pl.BlockSpec(memory_space=pltpu.VMEM)
    smem = pl.BlockSpec(memory_space=pltpu.SMEM)

    def buf(*shape, dtype=F32):
        return pltpu.VMEM(shape, dtype)

    scratch = [
        buf(2, ty, tx), buf(5, ext, tx), buf(5, ext, tx),
        buf(2 * tx, 2 * tx, dtype=BF16), buf(2 * tx, 2 * tx, dtype=BF16),
        buf(PACK, ext, 2 * tx), buf(levels, ext, tx),
        buf(groups + 2, ty, tx),
        buf(levels + 2, EDGE, tx), buf(levels + 2, EDGE, tx),
        buf(groups + 2, EDGE, tx), buf(groups + 2, EDGE, tx),
        buf(groups + 2, ty, tx), buf(groups + 2, ty, tx),
        buf(levels + 2, EDGE, tx), buf(levels + 2, EDGE, tx),
        buf(3, groups + 2, EDGE, tx), buf(3, groups + 2, EDGE, tx),
        buf(groups, ext, tx),
        buf(levels, EDGE, tx), buf(levels, EDGE, tx),
        buf(groups, EDGE, tx), buf(groups, EDGE, tx),
        buf(groups, ext, tx), buf(groups, ext, tx),
        buf(levels, EDGE, tx), buf(levels, EDGE, tx),
        buf(3, groups, EDGE, tx), buf(3, groups, EDGE, tx),
        pltpu.SemaphoreType.DMA((10,)), pltpu.SemaphoreType.DMA((10,)),
        pltpu.SemaphoreType.DMA((10 * groups,)), pltpu.SemaphoreType.DMA((10 * groups,)),
    ]
    return pl.pallas_call(
        functools.partial(kernel, levels),
        out_shape=(
            jax.ShapeDtypeStruct(control.shape, F32),
            jax.ShapeDtypeStruct(innovations.shape, F32),
        ),
        in_specs=[vmem] * 8 + [smem],
        out_specs=(vmem, vmem),
        scratch_shapes=scratch,
        compiler_params=pltpu.CompilerParams(
            collective_id=0, has_side_effects=True, vmem_limit_bytes=40 * 1024 * 1024
        ),
    )(control, diffusivity, land_mask, innovations, obs_sigma, obs_row, obs_col, obs_frac, obs_counts)


def solution(mesh):
    in_specs = (
        P(None, "lat", "lon"),
        P("lat", "lon"),
        P("lat", "lon"),
        P("lat", None, "lon"),
        P("lat", None, "lon"),
        P("lat", "lon"),
        P("lat", "lon"),
        P("lat", None, "lon"),
        P("lat", "lon"),
    )
    out_specs = (P(None, "lat", "lon"), P("lat", None, "lon"))
    return jax.shard_map(
        on_device, mesh=mesh, in_specs=in_specs, out_specs=out_specs, check_vma=False
    )
```

time: 129 us -> 40.4 us (0.31)
  the two profiles are of different devices: /device:TPU:1 before, /device:TPU:0 now
where the time goes in v1:
time: 40.4 us; the launch traced here: 40 us
  Pallas kernels  30.7 us (76%)
  local copies, waits for them, and re-layouts  7.96 us (20%)
  between operations  1.3 us (3%)
    pallas_call x1, Pallas kernels, on_device(): pl.pallas_call(functools.partial(kernel, levels), out_shape=(jax.ShapeDty...  30.7 us
    unnamed x18, local copies, waits for them, and re-layouts  7.96 us

profile of v1, /device:TPU:0, one launch (start us, length us, event | category | flops | bytes accessed | tf_op | source)
XLA Modules:
  0.0 40.0 jit_solution(14676179607962149626)
XLA Ops:
  1.3 0.0 copy-start
  1.3 1.3 %copy-done = f32[80,32,128]{2,1,0:T(8,128)S(1)} copy-done((f32[80,32,128]{2,1,0:T(8,128)S(1)}, f32[80,32,128]{2,1,0:T(8,128)}, u32[]{:S(2)}) %copy-start) | copy-done | bytes 1310744
  2.6 0.0 copy-start.1
  2.6 0.8 %copy-done.1 = f32[1,80,128]{2,1,0:T(8,128)S(1)} copy-done((f32[1,80,128]{2,1,0:T(8,128)S(1)}, f32[1,80,128]{2,1,0:T(8,128)}, u32[]{:S(2)}) %copy-start.1) | copy-done | bytes 40984
  3.4 0.0 copy-start.2
  3.4 0.8 %copy-done.2 = f32[1,80,128]{2,1,0:T(8,128)S(1)} copy-done((f32[1,80,128]{2,1,0:T(8,128)S(1)}, f32[1,80,128]{2,1,0:T(8,128)}, u32[]{:S(2)}) %copy-start.2) | copy-done | bytes 40984
  4.2 0.0 copy-start.3
  4.2 0.7 %copy-done.3 = f32[32,128]{1,0:T(8,128)S(1)} copy-done((f32[32,128]{1,0:T(8,128)S(1)}, f32[32,128]{1,0:T(8,128)}, u32[]{:S(2)}) %copy-start.3) | copy-done | bytes 16408
  4.9 0.0 copy-start.4
  4.9 0.7 %copy-done.4 = s32[32,128]{1,0:T(8,128)S(1)} copy-done((s32[32,128]{1,0:T(8,128)S(1)}, s32[32,128]{1,0:T(8,128)}, u32[]{:S(2)}) %copy-start.4) | copy-done | bytes 16408
  5.6 0.0 copy-start.5
  5.6 0.7 %copy-done.5 = f32[1,2,128]{2,1,0:T(2,128)S(1)} copy-done((f32[1,2,128]{2,1,0:T(2,128)S(1)}, f32[1,2,128]{2,1,0:T(2,128)}, u32[]{:S(2)}) %copy-start.5) | copy-done | bytes 1048
  6.3 0.0 copy-start.6
  6.3 0.7 %copy-done.6 = s32[1,128]{1,0:T(1,128)S(1)} copy-done((s32[1,128]{1,0:T(1,128)S(1)}, s32[1,128]{1,0:T(1,128)}, u32[]{:S(2)}) %copy-start.6) | copy-done | bytes 536
  6.9 0.0 copy-start.7
  6.9 0.7 %copy-done.7 = s32[1,128]{1,0:T(1,128)S(1)} copy-done((s32[1,128]{1,0:T(1,128)S(1)}, s32[1,128]{1,0:T(1,128)}, u32[]{:S(2)}) %copy-start.7) | copy-done | bytes 536
  7.6 30.7 %shard_map.104 = (f32[80,32,128]{2,1,0:T(8,128)S(1)}, f32[1,80,128]{2,1,0:T(8,128)S(1)}) custom-call(f32[80,32,128]{2,1,0:T(8,128)S(1)} %copy-done, f32[32,128]{1,0:T(8,128)S(1)} %copy-done.3, s32[32,128]{1,0:T(8,128)S(1)} %copy-done.4, f32[1,80,128]{2,1,0:T(8,128)S(1)} %copy-done.1, f32[1,80,128]{2,1,0:T(8,128)S(1)} %copy-done.2, s32[1,128]{1,0:T(1,128)S(1)} %copy-done.6, ...), custom_call_target="tpu_custom_call" | custom-call | tf_op jit(solution)/shard_map/pallas_call | solution.py:409
  38.3 1.1 %copy.14 = f32[80,32,128]{2,1,0:T(8,128)} copy(f32[80,32,128]{2,1,0:T(8,128)S(1)} %get-tuple-element.4) | data formatting | bytes 2621440
  39.4 0.6 %copy.15 = f32[1,80,128]{2,1,0:T(8,128)} copy(f32[1,80,128]{2,1,0:T(8,128)S(1)} %get-tuple-element.5) | data formatting | bytes 81920
Async XLA Ops:
  1.3 1.3 %copy-start = (f32[80,32,128]{2,1,0:T(8,128)S(1)}, f32[80,32,128]{2,1,0:T(8,128)}, u32[]{:S(2)}) copy-start(f32[80,32,128]{2,1,0:T(8,128)} %control.1) | copy-start | bytes 3932164
  2.6 0.8 %copy-start.1 = (f32[1,80,128]{2,1,0:T(8,128)S(1)}, f32[1,80,128]{2,1,0:T(8,128)}, u32[]{:S(2)}) copy-start(f32[1,80,128]{2,1,0:T(8,128)} %innovations.1) | copy-start | bytes 122884
  3.4 0.8 %copy-start.2 = (f32[1,80,128]{2,1,0:T(8,128)S(1)}, f32[1,80,128]{2,1,0:T(8,128)}, u32[]{:S(2)}) copy-start(f32[1,80,128]{2,1,0:T(8,128)} %sigma.1) | copy-start | bytes 122884
  4.2 0.7 %copy-start.3 = (f32[32,128]{1,0:T(8,128)S(1)}, f32[32,128]{1,0:T(8,128)}, u32[]{:S(2)}) copy-start(f32[32,128]{1,0:T(8,128)} %diffusivity.1) | copy-start | bytes 49156
  4.9 0.7 %copy-start.4 = (s32[32,128]{1,0:T(8,128)S(1)}, s32[32,128]{1,0:T(8,128)}, u32[]{:S(2)}) copy-start(s32[32,128]{1,0:T(8,128)} %land_mask.1) | copy-start | bytes 49156
  5.6 0.7 %copy-start.5 = (f32[1,2,128]{2,1,0:T(2,128)S(1)}, f32[1,2,128]{2,1,0:T(2,128)}, u32[]{:S(2)}) copy-start(f32[1,2,128]{2,1,0:T(2,128)} %frac.1) | copy-start | bytes 3076
  6.3 0.7 %copy-start.6 = (s32[1,128]{1,0:T(1,128)S(1)}, s32[1,128]{1,0:T(1,128)}, u32[]{:S(2)}) copy-start(s32[1,128]{1,0:T(1,128)} %obs_row.1) | copy-start | bytes 1540
  6.9 0.7 %copy-start.7 = (s32[1,128]{1,0:T(1,128)S(1)}, s32[1,128]{1,0:T(1,128)}, u32[]{:S(2)}) copy-start(s32[1,128]{1,0:T(1,128)} %obs_col.1) | copy-start | bytes 1540

commit v2 on v1

--- a/solution.py
+++ b/solution.py
@@ -17,12 +17,14 @@
 
 def kernel(
     levels,
-    control, diffusivity, land_mask, innovations, sigma, obs_row, obs_col, frac, counts,
+    control_in, diffusivity_in, land_mask_in, innovations_in, sigma_in,
+    obs_row_in, obs_col_in, frac_in, counts,
     gradient, departures,
+    control, diffusivity, land_mask, innovations, sigma, obs_row, obs_col, frac, local_sem,
     coeff, weights, strip_weights, hot_in, hot_out, work, adjoint,
-    pack, rows_up, rows_dn, prow_up, prow_dn,
-    pack_e, pack_w, got_up, got_dn, pgot_up, pgot_dn,
-    bpack, brow_up, brow_dn, bprow_up, bprow_dn,
+    pack, send_e, send_w, rows_up, rows_dn,
+    from_w, from_e, pack_e, pack_w, got_up, got_dn, pgot_up, pgot_dn,
+    bpack, brow_up, brow_dn,
     bpack_e, bpack_w, bgot_up, bgot_dn, bpgot_up, bpgot_dn,
     send_sem, recv_sem, bsend_sem, brecv_sem,
 ):
@@ -35,6 +37,28 @@
     has_up, has_dn = lat < n_lat - 1, lat > 0
     columns = (lon, east, west)
 
+    def fetch(src, dst, index):
+        return pltpu.make_async_copy(src, dst, local_sem.at[index])
+
+    def fetch_group(g):
+        mine = pl.ds(g * PACK, PACK)
+        return fetch(control_in.at[mine], control.at[mine], g)
+
+    small = [
+        fetch(src, dst, groups + i)
+        for i, (src, dst) in enumerate((
+            (diffusivity_in, diffusivity), (land_mask_in, land_mask),
+            (obs_row_in, obs_row), (obs_col_in, obs_col), (frac_in, frac),
+            (innovations_in, innovations), (sigma_in, sigma),
+        ))
+    ]
+    for c in small[:2]:
+        c.start()
+    for g in range(groups):
+        fetch_group(g).start()
+    for c in small[2:]:
+        c.start()
+
     barrier = pltpu.get_barrier_semaphore()
 
     def greet(x, y):
@@ -65,24 +89,12 @@
     slot = lax.rem(lane, SLOT)
     sub8 = lax.broadcasted_iota(jnp.int32, (8, tx), 0)
 
+    lane_t = lane[0:ty]
+    slot_t = slot[0:ty]
+    for c in small[:2]:
+        c.wait()
     coeff[0] = diffusivity[...]
     coeff[1] = land_mask[...].astype(F32)
-    rows_up[0:levels] = control[:, ty - EDGE : ty, :]
-    rows_dn[0:levels] = control[:, 0:EDGE, :]
-    rows_up[levels : levels + 2] = coeff[:, ty - EDGE : ty, :]
-    rows_dn[levels : levels + 2] = coeff[:, 0:EDGE, :]
-
-    lane_t = lane[0:ty]
-
-    def pack_group(g, carry):
-        acc = jnp.zeros((ty, tx), F32)
-        for p in range(PACK):
-            x = control[g * PACK + p]
-            acc = jnp.where(lane_t // SLOT == p, pltpu.roll(x, SLOT * p + 2, 1), acc)
-        pack[g] = acc
-        return carry
-
-    lax.fori_loop(0, groups, pack_group, 0)
     for k in range(2):
         base = jnp.where(lane_t < SLOT, pltpu.roll(coeff[k], 2, 1), 0.0)
         width = SLOT
@@ -90,8 +102,34 @@
             base = base + pltpu.roll(base, width, 1)
             width *= 2
         pack[groups + k] = base
-    prow_up[...] = pack[:, ty - EDGE : ty, :]
-    prow_dn[...] = pack[:, 0:EDGE, :]
+
+    def pack_group(g, carry):
+        fetch_group(g).wait()
+        acc = jnp.zeros((ty, tx), F32)
+        for p in range(PACK):
+            x = control[g * PACK + p]
+            acc = jnp.where(lane_t // SLOT == p, pltpu.roll(x, SLOT * p + 2, 1), acc)
+        pack[g] = acc
+        return carry
+
+    lax.fori_loop(0, groups, pack_group, 0)
+    for q in range(send_e.shape[0]):
+        acc = pack[4 * q]
+        for j in range(1, min(4, groups + 2 - 4 * q)):
+            acc = jnp.where(slot_t // 2 == j, pltpu.roll(pack[4 * q + j], 2 * j, 1), acc)
+        send_e[q] = acc
+    for q in range(send_w.shape[0]):
+        acc = pltpu.roll(pack[2 * q], tx - 2, 1)
+        if 2 * q + 1 < groups + 2:
+            acc = jnp.where(slot_t < 4, acc, pltpu.roll(pack[2 * q + 1], 2, 1))
+        send_w[q] = acc
+    rows_up[0:levels] = control[:, ty - EDGE : ty, :]
+    rows_dn[0:levels] = control[:, 0:EDGE, :]
+    rows_up[levels : levels + 2] = coeff[:, ty - EDGE : ty, :]
+    rows_dn[levels : levels + 2] = coeff[:, 0:EDGE, :]
+    rows_up[levels + 2 : levels + groups + 4] = pack[:, ty - EDGE : ty, :]
+    rows_dn[levels + 2 : levels + groups + 4] = pack[:, 0:EDGE, :]
+    packed = pl.ds(levels + 2, groups + 2)
 
     @pl.when(jnp.logical_and(has_up, has_dn))
     def _():
@@ -102,20 +140,20 @@
         pl.semaphore_wait(barrier, 5)
 
     side_copies = (
-        copy(pack, pack_w, send_sem, recv_sem, 0, east, lat),
-        copy(pack, pack_e, send_sem, recv_sem, 1, west, lat),
+        copy(send_e, from_w, send_sem, recv_sem, 0, east, lat),
+        copy(send_w, from_e, send_sem, recv_sem, 1, west, lat),
     )
 
     def up_copies():
         return [copy(rows_up, got_dn, send_sem, recv_sem, 2, lon, lat + 1)] + [
-            copy(prow_up, pgot_dn.at[place[i]], send_sem, recv_sem, 4 + i, columns[i], lat + 1)
-            for i in range(3)
+            copy(rows_up.at[packed], pgot_dn.at[place[i] - 1], send_sem, recv_sem, 3 + i, columns[i], lat + 1)
+            for i in (1, 2)
         ]
 
     def dn_copies():
         return [copy(rows_dn, got_up, send_sem, recv_sem, 3, lon, lat - 1)] + [
-            copy(prow_dn, pgot_up.at[place[i]], send_sem, recv_sem, 7 + i, columns[i], lat - 1)
-            for i in range(3)
+            copy(rows_dn.at[packed], pgot_up.at[place[i] - 1], send_sem, recv_sem, 5 + i, columns[i], lat - 1)
+            for i in (1, 2)
         ]
 
     for c in side_copies:
@@ -131,30 +169,41 @@
         for c in dn_copies():
             c.start()
 
+    for c in small[2:]:
+        c.wait()
     col = obs_col[...]
     row = obs_row[...]
+    frac_y = frac[0, 0:1, :]
+    frac_x = frac[0, 1:2, :]
     cell = lax.broadcasted_iota(jnp.int32, (tx, tx), 0)
     kind = lax.rem(cell, SLOT)
-
-    def hot(wanted):
-        return jnp.concatenate(
-            [jnp.where(col == wanted, 1.0, 0.0), jnp.where(col + 1 == wanted, 1.0, 0.0)], axis=1
-        ).astype(BF16)
-
-    main_hot = hot(cell)
-    hot_in[0:tx] = main_hot
-    hot_in[tx : 2 * tx] = hot(jnp.where(kind == 2, tx, -9))
+    picks = jnp.concatenate(
+        [jnp.where(col == cell, 1.0, 0.0), jnp.where(col + 1 == cell, 1.0, 0.0)], axis=1
+    ).astype(BF16)
+    hot_in[0:tx] = picks
+    hot_in[tx : 2 * tx] = picks
+
+    def parts(x):
+        a = x.astype(BF16)
+        rest = x - a.astype(F32)
+        b = rest.astype(BF16)
+        return a, b, (rest - b.astype(F32)).astype(BF16)
+
     chosen = jnp.where(
         kind < 3, tx - 2 + kind, jnp.where(kind == 5, 0, jnp.where(kind == 6, 1, jnp.where(kind == 7, 0, -9)))
     )
-    hot_out[0:tx] = main_hot
-    hot_out[tx : 2 * tx] = hot(chosen)
-
-    frac_y = frac[0, 0:1, :]
-    frac_x = frac[0, 1:2, :]
+    for i, wanted in enumerate((cell, chosen)):
+        share = jnp.where(col == wanted, 1.0 - frac_x, 0.0) + jnp.where(col + 1 == wanted, frac_x, 0.0)
+        high, mid, low = parts(share)
+        there = pl.ds(i * tx, tx)
+        hot_out[0, there] = jnp.concatenate([high, high], axis=1)
+        hot_out[1, there] = jnp.concatenate([mid, mid], axis=1)
+        hot_out[2, there] = jnp.concatenate([low, high], axis=1)
+
     line = lax.broadcasted_iota(jnp.int32, (ext, tx), 0)
     row_weight = jnp.where(line == row, 1.0 - frac_y, 0.0) + jnp.where(line == row + 1, frac_y, 0.0)
     row_weight = jnp.where(jnp.logical_and(line == ty, lat == n_lat - 1), 0.0, row_weight)
+    beyond = row_weight * jnp.where(col == tx - 1, frac_x, 0.0)
     live = lax.broadcasted_iota(jnp.int32, (PACK, tx), 1) < counts[0, 0]
 
     for c in side_copies:
@@ -184,11 +233,19 @@
         got_dn[...] = jnp.zeros_like(got_dn)
         pgot_dn[...] = jnp.zeros_like(pgot_dn)
 
+    for k in range(groups + 2):
+        q, j = divmod(k, 4)
+        pack_w[k] = pltpu.roll(from_w[q], (5 - 2 * j) % tx, 1)
+        q, j = divmod(k, 2)
+        pack_e[k] = pltpu.roll(from_e[q], tx - 2 if j else 2, 1)
+
     def strip_of(k):
-        own = jnp.concatenate([pack[k], pgot_up[0, k], pgot_dn[0, k]], axis=0)
-        e = jnp.concatenate([pack_e[k], pgot_up[1, k], pgot_dn[1, k]], axis=0)
-        w = jnp.concatenate([pack_w[k], pgot_up[2, k], pgot_dn[2, k]], axis=0)
-        far = jnp.where(slot == 7, pltpu.roll(own, 5, 1), pltpu.roll(w, 5, 1))
+        at = levels + 2 + k
+        own = jnp.concatenate([pack[k], got_up[at], got_dn[at]], axis=0)
+        e = jnp.concatenate([pack_e[k], pgot_up[0, k], pgot_dn[0, k]], axis=0)
+        w_rows = pltpu.roll(jnp.concatenate([pgot_up[1, k], pgot_dn[1, k]], axis=0), 5, 1)
+        w = jnp.concatenate([pack_w[k], w_rows], axis=0)
+        far = jnp.where(slot == 7, pltpu.roll(own, 5, 1), w)
         return jnp.where(slot < 2, own, jnp.where(slot < 5, e, far))
 
     def edge_of(strip):
@@ -231,37 +288,25 @@
             out = out + w[i] * near[i]
         return out
 
-    def parts(x):
-        a = x.astype(BF16)
-        rest = x - a.astype(F32)
-        b = rest.astype(BF16)
-        return a, b, (rest - b.astype(F32)).astype(BF16)
-
-    def dot(x, y, dims):
-        total = None
-        for part in parts(x):
-            one = lax.dot_general(part, y, (dims, ((), ())), preferred_element_type=F32)
-            total = one if total is None else total + one
-        return total
+    def dot(x, y, dims, precision=None):
+        return lax.dot_general(x, y, (dims, ((), ())), precision=precision, preferred_element_type=F32)
 
     def back_sides(g):
         return (
-            copy(bpack.at[g], bpack_w.at[g], bsend_sem, brecv_sem, g * 10, east, lat),
-            copy(bpack.at[g], bpack_e.at[g], bsend_sem, brecv_sem, g * 10 + 1, west, lat),
+            copy(bpack.at[g], bpack_w.at[g], bsend_sem, brecv_sem, g * 8, east, lat),
+            copy(bpack.at[g], bpack_e.at[g], bsend_sem, brecv_sem, g * 8 + 1, west, lat),
         )
 
     def back_up(g):
-        mine = pl.ds(g * PACK, PACK)
-        return [copy(brow_up.at[mine], bgot_dn.at[mine], bsend_sem, brecv_sem, g * 10 + 2, lon, lat + 1)] + [
-            copy(bprow_up.at[g], bpgot_dn.at[place[i], g], bsend_sem, brecv_sem, g * 10 + 4 + i, columns[i], lat + 1)
-            for i in range(3)
+        return [copy(brow_up.at[g], bgot_dn.at[g], bsend_sem, brecv_sem, g * 8 + 2, lon, lat + 1)] + [
+            copy(brow_up.at[g, PACK], bpgot_dn.at[place[i] - 1, g], bsend_sem, brecv_sem, g * 8 + 3 + i, columns[i], lat + 1)
+            for i in (1, 2)
         ]
 
     def back_dn(g):
-        mine = pl.ds(g * PACK, PACK)
-        return [copy(brow_dn.at[mine], bgot_up.at[mine], bsend_sem, brecv_sem, g * 10 + 3, lon, lat - 1)] + [
-            copy(bprow_dn.at[g], bpgot_up.at[place[i], g], bsend_sem, brecv_sem, g * 10 + 7 + i, columns[i], lat - 1)
-            for i in range(3)
+        return [copy(brow_dn.at[g], bgot_up.at[g], bsend_sem, brecv_sem, g * 8 + 3, lon, lat - 1)] + [
+            copy(brow_dn.at[g, PACK], bpgot_up.at[place[i] - 1, g], bsend_sem, brecv_sem, g * 8 + 5 + i, columns[i], lat - 1)
+            for i in (1, 2)
         ]
 
     def forward(g, carry):
@@ -275,30 +320,34 @@
             x = jnp.concatenate([control[level], got_up[level], got_dn[level]], axis=0)
             x = diffuse(x, fill_of(edge0, p), weights)
             x = diffuse(x, fill_of(edge1, p), weights)
-            work[p, :, 0:tx] = x
-            work[p, :, tx : 2 * tx] = jnp.where(lane // SLOT == p, strip2, 0.0)
-        picked = dot(work[...].reshape(PACK * ext, 2 * tx), hot_in[...], ((1,), (0,)))
+            work[p] = x
+        high, mid, low = parts(work[...].reshape(PACK * ext, tx))
+        picked = dot(jnp.concatenate([high, mid], axis=1), hot_in[...], ((1,), (0,)))
+        picked = picked + dot(low, hot_in[0:tx], ((1,), (0,)))
+        outer = dot(strip2, beyond, ((0,), (0,)), lax.Precision.HIGHEST)
+        outer = jnp.sum(jnp.where(sub8[None] == 2, outer.reshape(PACK, SLOT, tx), 0.0), axis=1)
         mixed = picked[:, 0:tx] * (1.0 - frac_x) + picked[:, tx : 2 * tx] * frac_x
-        sample = jnp.sum(mixed.reshape(PACK, ext, tx) * row_weight[None], axis=1)
+        sample = jnp.sum(mixed.reshape(PACK, ext, tx) * row_weight[None], axis=1) + outer
         mine = pl.ds(g * PACK, PACK)
         departure = jnp.where(live, sample - innovations[0, mine, :], 0.0)
         departures[0, mine, :] = departure
         s = sigma[0, mine, :]
         weighted = departure / (s * s)
-        spread = weighted[:, None, :] * row_weight[None]
-        work[:, :, 0:tx] = spread * (1.0 - frac_x)[None]
-        work[:, :, tx : 2 * tx] = spread * frac_x[None]
-        field = dot(work[...].reshape(PACK * ext, 2 * tx), hot_out[...], ((1,), (1,)))
+        spread = (weighted[:, None, :] * row_weight[None]).reshape(PACK * ext, tx)
+        high, mid, low = parts(spread)
+        upper = jnp.concatenate([high, mid], axis=1)
+        field = dot(upper, hot_out[0], ((1,), (1,))) + dot(upper, hot_out[1], ((1,), (1,)))
+        field = field + dot(jnp.concatenate([high, low], axis=1), hot_out[2], ((1,), (1,)))
         adjoint[mine] = field[:, 0:tx].reshape(PACK, ext, tx)
         sides = field[:, tx : 2 * tx].reshape(PACK, ext, tx)
         acc = sides[0]
         for p in range(1, PACK):
             acc = jnp.where(lane // SLOT == p, sides[p], acc)
         bpack[g] = acc
-        brow_up[mine] = adjoint[mine, ty - 3 : ty + 1, :]
-        brow_dn[mine] = adjoint[mine, 0:EDGE, :]
-        bprow_up[g] = bpack[g, ty - 3 : ty + 1, :]
-        bprow_dn[g] = bpack[g, 0:EDGE, :]
+        brow_up[g, 0:PACK] = adjoint[mine, ty - 3 : ty + 1, :]
+        brow_dn[g, 0:PACK] = adjoint[mine, 0:EDGE, :]
+        brow_up[g, PACK] = bpack[g, ty - 3 : ty + 1, :]
+        brow_dn[g, PACK] = bpack[g, 0:EDGE, :]
         for c in back_sides(g):
             c.start()
 
@@ -351,20 +400,20 @@
             for c in back_up(g):
                 c.wait_recv()
 
-        own = with_rows(bpack[g], bpgot_up[0, g], bpgot_dn[0, g])
-        e = with_rows(bpack_e[g], bpgot_up[1, g], bpgot_dn[1, g])
-        w = with_rows(bpack_w[g], bpgot_up[2, g], bpgot_dn[2, g])
-        from_e = pltpu.roll(e, tx - 3, 1)
-        from_w = pltpu.roll(w, 5, 1)
+        own = with_rows(bpack[g], bgot_up[g, PACK], bgot_dn[g, PACK])
+        e = with_rows(bpack_e[g], bpgot_up[0, g], bpgot_dn[0, g])
+        w = with_rows(bpack_w[g], bpgot_up[1, g], bpgot_dn[1, g])
+        side_e = pltpu.roll(e, tx - 3, 1)
+        side_w = pltpu.roll(w, 5, 1)
         strip = jnp.where(jnp.logical_or(slot < 3, slot == 7), own, 0.0)
-        strip = strip + jnp.where(jnp.logical_or(slot == 2, slot == 3), from_e, 0.0)
-        strip = strip + jnp.where(slot > 4, from_w, 0.0)
-        first_col = jnp.where(slot == 7, from_w, 0.0)
+        strip = strip + jnp.where(jnp.logical_or(slot == 2, slot == 3), side_e, 0.0)
+        strip = strip + jnp.where(slot > 4, side_w, 0.0)
+        first_col = jnp.where(slot == 7, side_w, 0.0)
         edge0 = edge_of(strip)
         edge1 = edge_of(diffuse(strip, None, strip_weights))
         for p in range(PACK):
             level = g * PACK + p
-            x = with_rows(adjoint[level], bgot_up[level], bgot_dn[level])
+            x = with_rows(adjoint[level], bgot_up[g, p], bgot_dn[g, p])
             extra = pltpu.roll(first_col, (tx - 7 - SLOT * p) % tx, 1)
             x = x + jnp.where(lane == 0, extra, 0.0)
             x = diffuse(x, fill_of(edge0, p), weights)
@@ -387,24 +436,28 @@
     def buf(*shape, dtype=F32):
         return pltpu.VMEM(shape, dtype)
 
+    four, two = -(-(groups + 2) // 4), -(-(groups + 2) // 2)
+    rows = levels + groups + 4
     scratch = [
+        buf(levels, ty, tx), buf(ty, tx), buf(ty, tx, dtype=jnp.int32),
+        buf(*innovations.shape), buf(*obs_sigma.shape),
+        buf(*obs_row.shape, dtype=jnp.int32), buf(*obs_col.shape, dtype=jnp.int32), buf(*obs_frac.shape),
+        pltpu.SemaphoreType.DMA((groups + 7,)),
         buf(2, ty, tx), buf(5, ext, tx), buf(5, ext, tx),
-        buf(2 * tx, 2 * tx, dtype=BF16), buf(2 * tx, 2 * tx, dtype=BF16),
-        buf(PACK, ext, 2 * tx), buf(levels, ext, tx),
-        buf(groups + 2, ty, tx),
-        buf(levels + 2, EDGE, tx), buf(levels + 2, EDGE, tx),
-        buf(groups + 2, EDGE, tx), buf(groups + 2, EDGE, tx),
-        buf(groups + 2, ty, tx), buf(groups + 2, ty, tx),
-        buf(levels + 2, EDGE, tx), buf(levels + 2, EDGE, tx),
-        buf(3, groups + 2, EDGE, tx), buf(3, groups + 2, EDGE, tx),
+        buf(2 * tx, 2 * tx, dtype=BF16), buf(3, 2 * tx, 2 * tx, dtype=BF16),
+        buf(PACK, ext, tx), buf(levels, ext, tx),
+        buf(groups + 2, ty, tx), buf(four, ty, tx), buf(two, ty, tx),
+        buf(rows, EDGE, tx), buf(rows, EDGE, tx),
+        buf(four, ty, tx), buf(two, ty, tx), buf(groups + 2, ty, tx), buf(groups + 2, ty, tx),
+        buf(rows, EDGE, tx), buf(rows, EDGE, tx),
+        buf(2, groups + 2, EDGE, tx), buf(2, groups + 2, EDGE, tx),
         buf(groups, ext, tx),
-        buf(levels, EDGE, tx), buf(levels, EDGE, tx),
-        buf(groups, EDGE, tx), buf(groups, EDGE, tx),
+        buf(groups, PACK + 1, EDGE, tx), buf(groups, PACK + 1, EDGE, tx),
         buf(groups, ext, tx), buf(groups, ext, tx),
-        buf(levels, EDGE, tx), buf(levels, EDGE, tx),
-        buf(3, groups, EDGE, tx), buf(3, groups, EDGE, tx),
-        pltpu.SemaphoreType.DMA((10,)), pltpu.SemaphoreType.DMA((10,)),
-        pltpu.SemaphoreType.DMA((10 * groups,)), pltpu.SemaphoreType.DMA((10 * groups,)),
+        buf(groups, PACK + 1, EDGE, tx), buf(groups, PACK + 1, EDGE, tx),
+        buf(2, groups, EDGE, tx), buf(2, groups, EDGE, tx),
+        pltpu.SemaphoreType.DMA((8,)), pltpu.SemaphoreType.DMA((8,)),
+        pltpu.SemaphoreType.DMA((8 * groups,)), pltpu.SemaphoreType.DMA((8 * groups,)),
     ]
     return pl.pallas_call(
         functools.partial(kernel, levels),
@@ -412,7 +465,7 @@
             jax.ShapeDtypeStruct(control.shape, F32),
             jax.ShapeDtypeStruct(innovations.shape, F32),
         ),
-        in_specs=[vmem] * 8 + [smem],
+        in_specs=[pl.BlockSpec(memory_space=pltpu.HBM)] * 8 + [smem],
         out_specs=(vmem, vmem),
         scratch_shapes=scratch,
         compiler_params=pltpu.CompilerParams(

time: 40.4 us -> 37.7 us (0.933)
  the two profiles are of different devices: /device:TPU:0 before, /device:TPU:1 now
where the time goes in v2:
time: 37.7 us; the launch traced here: 37.3 us
  Pallas kernels  28 us (74%)
  local copies, waits for them, and re-layouts  7.96 us (21%)
  between operations  1.3 us (3%)
    pallas_call x1, Pallas kernels, on_device(): pl.pallas_call(functools.partial(kernel, levels), out_shape=(jax.ShapeDty...  28 us
    unnamed x18, local copies, waits for them, and re-layouts  7.96 us

profile of v2, /device:TPU:1, one launch (start us, length us, event | category | flops | bytes accessed | tf_op | source)
XLA Modules:
  0.0 37.3 jit_solution(11469070676196490595)
XLA Ops:
  1.3 0.0 copy-start
  1.3 1.3 %copy-done = f32[80,32,128]{2,1,0:T(8,128)S(1)} copy-done((f32[80,32,128]{2,1,0:T(8,128)S(1)}, f32[80,32,128]{2,1,0:T(8,128)}, u32[]{:S(2)}) %copy-start) | copy-done | bytes 1310744
  2.6 0.0 copy-start.1
  2.6 0.8 %copy-done.1 = f32[1,80,128]{2,1,0:T(8,128)S(1)} copy-done((f32[1,80,128]{2,1,0:T(8,128)S(1)}, f32[1,80,128]{2,1,0:T(8,128)}, u32[]{:S(2)}) %copy-start.1) | copy-done | bytes 40984
  3.4 0.0 copy-start.2
  3.4 0.8 %copy-done.2 = f32[1,80,128]{2,1,0:T(8,128)S(1)} copy-done((f32[1,80,128]{2,1,0:T(8,128)S(1)}, f32[1,80,128]{2,1,0:T(8,128)}, u32[]{:S(2)}) %copy-start.2) | copy-done | bytes 40984
  4.2 0.0 copy-start.3
  4.2 0.7 %copy-done.3 = f32[32,128]{1,0:T(8,128)S(1)} copy-done((f32[32,128]{1,0:T(8,128)S(1)}, f32[32,128]{1,0:T(8,128)}, u32[]{:S(2)}) %copy-start.3) | copy-done | bytes 16408
  4.9 0.0 copy-start.4
  4.9 0.7 %copy-done.4 = s32[32,128]{1,0:T(8,128)S(1)} copy-done((s32[32,128]{1,0:T(8,128)S(1)}, s32[32,128]{1,0:T(8,128)}, u32[]{:S(2)}) %copy-start.4) | copy-done | bytes 16408
  5.6 0.0 copy-start.5
  5.6 0.7 %copy-done.5 = f32[1,2,128]{2,1,0:T(2,128)S(1)} copy-done((f32[1,2,128]{2,1,0:T(2,128)S(1)}, f32[1,2,128]{2,1,0:T(2,128)}, u32[]{:S(2)}) %copy-start.5) | copy-done | bytes 1048
  6.3 0.0 copy-start.6
  6.3 0.7 %copy-done.6 = s32[1,128]{1,0:T(1,128)S(1)} copy-done((s32[1,128]{1,0:T(1,128)S(1)}, s32[1,128]{1,0:T(1,128)}, u32[]{:S(2)}) %copy-start.6) | copy-done | bytes 536
  6.9 0.0 copy-start.7
  6.9 0.7 %copy-done.7 = s32[1,128]{1,0:T(1,128)S(1)} copy-done((s32[1,128]{1,0:T(1,128)S(1)}, s32[1,128]{1,0:T(1,128)}, u32[]{:S(2)}) %copy-start.7) | copy-done | bytes 536
  7.6 28.0 %shard_map.104 = (f32[80,32,128]{2,1,0:T(8,128)S(1)}, f32[1,80,128]{2,1,0:T(8,128)S(1)}) custom-call(f32[80,32,128]{2,1,0:T(8,128)S(1)} %copy-done, f32[32,128]{1,0:T(8,128)S(1)} %copy-done.3, s32[32,128]{1,0:T(8,128)S(1)} %copy-done.4, f32[1,80,128]{2,1,0:T(8,128)S(1)} %copy-done.1, f32[1,80,128]{2,1,0:T(8,128)S(1)} %copy-done.2, s32[1,128]{1,0:T(1,128)S(1)} %copy-done.6, ...), custom_call_target="tpu_custom_call" | custom-call | tf_op jit(solution)/shard_map/pallas_call | solution.py:462
  35.6 1.1 %copy.14 = f32[80,32,128]{2,1,0:T(8,128)} copy(f32[80,32,128]{2,1,0:T(8,128)S(1)} %get-tuple-element.4) | data formatting | bytes 2621440
  36.7 0.6 %copy.15 = f32[1,80,128]{2,1,0:T(8,128)} copy(f32[1,80,128]{2,1,0:T(8,128)S(1)} %get-tuple-element.5) | data formatting | bytes 81920
Async XLA Ops:
  1.3 1.3 %copy-start = (f32[80,32,128]{2,1,0:T(8,128)S(1)}, f32[80,32,128]{2,1,0:T(8,128)}, u32[]{:S(2)}) copy-start(f32[80,32,128]{2,1,0:T(8,128)} %control_in.1) | copy-start | bytes 3932164
  2.6 0.8 %copy-start.1 = (f32[1,80,128]{2,1,0:T(8,128)S(1)}, f32[1,80,128]{2,1,0:T(8,128)}, u32[]{:S(2)}) copy-start(f32[1,80,128]{2,1,0:T(8,128)} %innovations_in.1) | copy-start | bytes 122884
  3.4 0.8 %copy-start.2 = (f32[1,80,128]{2,1,0:T(8,128)S(1)}, f32[1,80,128]{2,1,0:T(8,128)}, u32[]{:S(2)}) copy-start(f32[1,80,128]{2,1,0:T(8,128)} %sigma_in.1) | copy-start | bytes 122884
  4.2 0.7 %copy-start.3 = (f32[32,128]{1,0:T(8,128)S(1)}, f32[32,128]{1,0:T(8,128)}, u32[]{:S(2)}) copy-start(f32[32,128]{1,0:T(8,128)} %diffusivity_in.1) | copy-start | bytes 49156
  4.9 0.7 %copy-start.4 = (s32[32,128]{1,0:T(8,128)S(1)}, s32[32,128]{1,0:T(8,128)}, u32[]{:S(2)}) copy-start(s32[32,128]{1,0:T(8,128)} %land_mask_in.1) | copy-start | bytes 49156
  5.6 0.7 %copy-start.5 = (f32[1,2,128]{2,1,0:T(2,128)S(1)}, f32[1,2,128]{2,1,0:T(2,128)}, u32[]{:S(2)}) copy-start(f32[1,2,128]{2,1,0:T(2,128)} %frac_in.1) | copy-start | bytes 3076
  6.3 0.7 %copy-start.6 = (s32[1,128]{1,0:T(1,128)S(1)}, s32[1,128]{1,0:T(1,128)}, u32[]{:S(2)}) copy-start(s32[1,128]{1,0:T(1,128)} %obs_row_in.1) | copy-start | bytes 1540
  6.9 0.7 %copy-start.7 = (s32[1,128]{1,0:T(1,128)S(1)}, s32[1,128]{1,0:T(1,128)}, u32[]{:S(2)}) copy-start(s32[1,128]{1,0:T(1,128)} %obs_col_in.1) | copy-start | bytes 1540

commit v3 on v2

--- a/solution.py
+++ b/solution.py
@@ -180,8 +180,8 @@
     picks = jnp.concatenate(
         [jnp.where(col == cell, 1.0, 0.0), jnp.where(col + 1 == cell, 1.0, 0.0)], axis=1
     ).astype(BF16)
-    hot_in[0:tx] = picks
-    hot_in[tx : 2 * tx] = picks
+    for i in range(3):
+        hot_in[i * tx : (i + 1) * tx] = picks
 
     def parts(x):
         a = x.astype(BF16)
@@ -194,11 +194,9 @@
     )
     for i, wanted in enumerate((cell, chosen)):
         share = jnp.where(col == wanted, 1.0 - frac_x, 0.0) + jnp.where(col + 1 == wanted, frac_x, 0.0)
-        high, mid, low = parts(share)
-        there = pl.ds(i * tx, tx)
-        hot_out[0, there] = jnp.concatenate([high, high], axis=1)
-        hot_out[1, there] = jnp.concatenate([mid, mid], axis=1)
-        hot_out[2, there] = jnp.concatenate([low, high], axis=1)
+        high, mid, low = parts(share.T)
+        for k, part in enumerate((high, high, mid, mid, low, high)):
+            hot_out[k * tx : (k + 1) * tx, i * tx : (i + 1) * tx] = part
 
     line = lax.broadcasted_iota(jnp.int32, (ext, tx), 0)
     row_weight = jnp.where(line == row, 1.0 - frac_y, 0.0) + jnp.where(line == row + 1, frac_y, 0.0)
@@ -315,15 +313,16 @@
         strip1 = diffuse(strip0, None, strip_weights)
         edge1 = edge_of(strip1)
         strip2 = diffuse(strip1, None, strip_weights)
-        for p in range(PACK):
-            level = g * PACK + p
-            x = jnp.concatenate([control[level], got_up[level], got_dn[level]], axis=0)
-            x = diffuse(x, fill_of(edge0, p), weights)
-            x = diffuse(x, fill_of(edge1, p), weights)
-            work[p] = x
-        high, mid, low = parts(work[...].reshape(PACK * ext, tx))
-        picked = dot(jnp.concatenate([high, mid], axis=1), hot_in[...], ((1,), (0,)))
-        picked = picked + dot(low, hot_in[0:tx], ((1,), (0,)))
+        for p in range(0, PACK, 2):
+            pair = []
+            for q in (p, p + 1):
+                level = g * PACK + q
+                x = jnp.concatenate([control[level], got_up[level], got_dn[level]], axis=0)
+                x = diffuse(x, fill_of(edge0, q), weights)
+                pair.append(diffuse(x, fill_of(edge1, q), weights))
+            for k, part in enumerate(parts(jnp.concatenate(pair, axis=0))):
+                work[p * ext : (p + 2) * ext, k * tx : (k + 1) * tx] = part
+        picked = dot(work[...], hot_in[...], ((1,), (0,)))
         outer = dot(strip2, beyond, ((0,), (0,)), lax.Precision.HIGHEST)
         outer = jnp.sum(jnp.where(sub8[None] == 2, outer.reshape(PACK, SLOT, tx), 0.0), axis=1)
         mixed = picked[:, 0:tx] * (1.0 - frac_x) + picked[:, tx : 2 * tx] * frac_x
@@ -335,9 +334,8 @@
         weighted = departure / (s * s)
         spread = (weighted[:, None, :] * row_weight[None]).reshape(PACK * ext, tx)
         high, mid, low = parts(spread)
-        upper = jnp.concatenate([high, mid], axis=1)
-        field = dot(upper, hot_out[0], ((1,), (1,))) + dot(upper, hot_out[1], ((1,), (1,)))
-        field = field + dot(jnp.concatenate([high, low], axis=1), hot_out[2], ((1,), (1,)))
+        spread = jnp.concatenate([high, mid, high, mid, high, low], axis=1)
+        field = dot(spread, hot_out[...], ((1,), (0,)))
         adjoint[mine] = field[:, 0:tx].reshape(PACK, ext, tx)
         sides = field[:, tx : 2 * tx].reshape(PACK, ext, tx)
         acc = sides[0]
@@ -431,7 +429,6 @@
     ext = ty + 8
     groups = levels // PACK
     vmem = pl.BlockSpec(memory_space=pltpu.VMEM)
-    smem = pl.BlockSpec(memory_space=pltpu.SMEM)
 
     def buf(*shape, dtype=F32):
         return pltpu.VMEM(shape, dtype)
@@ -444,8 +441,8 @@
         buf(*obs_row.shape, dtype=jnp.int32), buf(*obs_col.shape, dtype=jnp.int32), buf(*obs_frac.shape),
         pltpu.SemaphoreType.DMA((groups + 7,)),
         buf(2, ty, tx), buf(5, ext, tx), buf(5, ext, tx),
-        buf(2 * tx, 2 * tx, dtype=BF16), buf(3, 2 * tx, 2 * tx, dtype=BF16),
-        buf(PACK, ext, tx), buf(levels, ext, tx),
+        buf(3 * tx, 2 * tx, dtype=BF16), buf(6 * tx, 2 * tx, dtype=BF16),
+        buf(PACK * ext, 3 * tx, dtype=BF16), buf(levels, ext, tx),
         buf(groups + 2, ty, tx), buf(four, ty, tx), buf(two, ty, tx),
         buf(rows, EDGE, tx), buf(rows, EDGE, tx),
         buf(four, ty, tx), buf(two, ty, tx), buf(groups + 2, ty, tx), buf(groups + 2, ty, tx),
@@ -465,13 +462,18 @@
             jax.ShapeDtypeStruct(control.shape, F32),
             jax.ShapeDtypeStruct(innovations.shape, F32),
         ),
-        in_specs=[pl.BlockSpec(memory_space=pltpu.HBM)] * 8 + [smem],
+        in_specs=[pl.BlockSpec(memory_space=pltpu.HBM)] * 8 + [pl.BlockSpec(memory_space=pltpu.SMEM)],
         out_specs=(vmem, vmem),
         scratch_shapes=scratch,
         compiler_params=pltpu.CompilerParams(
             collective_id=0, has_side_effects=True, vmem_limit_bytes=40 * 1024 * 1024
         ),
-    )(control, diffusivity, land_mask, innovations, obs_sigma, obs_row, obs_col, obs_frac, obs_counts)
+    )(*(
+        pltpu.with_memory_space_constraint(a, pltpu.HBM)
+        for a in (
+            control, diffusivity, land_mask, innovations, obs_sigma, obs_row, obs_col, obs_frac
+        )
+    ), obs_counts)
 
 
 def solution(mesh):

time: 37.7 us -> 31.7 us (0.84)
  local copies, waits for them, and re-layouts: 7.96 us -> 1.68 us
  Pallas kernels: 28 us -> 28.5 us
    unnamed x18 -> x2, local copies, waits for them, and re-layouts: 7.96 us -> 1.68 us
    pallas_call x1, Pallas kernels: 28 us -> 28.5 us  [on_device(): pl.pallas_call(functools.partial(kernel, levels), out_shape=(jax.ShapeDty...]
where the time goes in v3:
time: 31.7 us; the launch traced here: 31.4 us
  Pallas kernels  28.5 us (90%)
  local copies, waits for them, and re-layouts  1.68 us (5%)
  between operations  1.29 us (4%)
    pallas_call x1, Pallas kernels, on_device(): pl.pallas_call(functools.partial(kernel, levels), out_shape=(jax.ShapeDty...  28.5 us
    unnamed x2, local copies, waits for them, and re-layouts  1.68 us

profile of v3, /device:TPU:1, one launch (start us, length us, event | category | flops | bytes accessed | tf_op | source)
XLA Modules:
  0.0 31.4 jit_solution(17936659410042363687)
XLA Ops:
  1.3 28.5 %shard_map.104 = (f32[80,32,128]{2,1,0:T(8,128)S(1)}, f32[1,80,128]{2,1,0:T(8,128)S(1)}) custom-call(f32[80,32,128]{2,1,0:T(8,128)} %control_in.1, f32[32,128]{1,0:T(8,128)} %diffusivity_in.1, s32[32,128]{1,0:T(8,128)} %land_mask_in.1, f32[1,80,128]{2,1,0:T(8,128)} %innovations_in.1, f32[1,80,128]{2,1,0:T(8,128)} %sigma_in.1, s32[1,128]{1,0:T(1,128)} %obs_row_in.1, ...), custom_call_target="tpu_custom_call" | custom-call | tf_op jit(solution)/shard_map/pallas_call | solution.py:459
  29.8 1.1 %copy.14 = f32[80,32,128]{2,1,0:T(8,128)} copy(f32[80,32,128]{2,1,0:T(8,128)S(1)} %get-tuple-element.4) | data formatting | bytes 2621440
  30.8 0.6 %copy.15 = f32[1,80,128]{2,1,0:T(8,128)} copy(f32[1,80,128]{2,1,0:T(8,128)S(1)} %get-tuple-element.5) | data formatting | bytes 81920

commit v4 on v3

--- a/solution.py
+++ b/solution.py
@@ -21,7 +21,7 @@
     obs_row_in, obs_col_in, frac_in, counts,
     gradient, departures,
     control, diffusivity, land_mask, innovations, sigma, obs_row, obs_col, frac, local_sem,
-    coeff, weights, strip_weights, hot_in, hot_out, work, adjoint,
+    coeff, weights, strip_weights, hot_in, hot_out, work, shift, adjoint,
     pack, send_e, send_w, rows_up, rows_dn,
     from_w, from_e, pack_e, pack_w, got_up, got_dn, pgot_up, pgot_dn,
     bpack, brow_up, brow_dn,
@@ -279,8 +279,19 @@
         around(mask, fill_of(edge_of(mask_strip), 0)),
     )
 
-    def diffuse(x, fill, w):
-        near = around(x, fill)
+    def shifted_rows(x, place):
+        place[8 : 8 + ext] = x
+        place[0:8] = x[ty:ext]
+        place[8 + ext : 16 + ext] = x[0:8]
+        return place[7 : 7 + ext], place[9 : 9 + ext]
+
+    def diffuse(x, fill, w, place=None):
+        if place is None:
+            near = around(x, fill)
+        else:
+            left = jnp.where(lane == 0, fill, pltpu.roll(x, 1, 1))
+            right = jnp.where(lane == tx - 1, fill, pltpu.roll(x, tx - 1, 1))
+            near = (left, right) + shifted_rows(x, place)
         out = w[4] * x
         for i in range(4):
             out = out + w[i] * near[i]
@@ -318,8 +329,8 @@
             for q in (p, p + 1):
                 level = g * PACK + q
                 x = jnp.concatenate([control[level], got_up[level], got_dn[level]], axis=0)
-                x = diffuse(x, fill_of(edge0, q), weights)
-                pair.append(diffuse(x, fill_of(edge1, q), weights))
+                x = diffuse(x, fill_of(edge0, q), weights, shift.at[q, 0])
+                pair.append(diffuse(x, fill_of(edge1, q), weights, shift.at[q, 1]))
             for k, part in enumerate(parts(jnp.concatenate(pair, axis=0))):
                 work[p * ext : (p + 2) * ext, k * tx : (k + 1) * tx] = part
         picked = dot(work[...], hot_in[...], ((1,), (0,)))
@@ -414,8 +425,8 @@
             x = with_rows(adjoint[level], bgot_up[g, p], bgot_dn[g, p])
             extra = pltpu.roll(first_col, (tx - 7 - SLOT * p) % tx, 1)
             x = x + jnp.where(lane == 0, extra, 0.0)
-            x = diffuse(x, fill_of(edge0, p), weights)
-            x = diffuse(x, fill_of(edge1, p), weights)
+            x = diffuse(x, fill_of(edge0, p), weights, shift.at[p, 0])
+            x = diffuse(x, fill_of(edge1, p), weights, shift.at[p, 1])
             gradient[level] = x[0:ty]
         return carry
 
@@ -442,7 +453,7 @@
         pltpu.SemaphoreType.DMA((groups + 7,)),
         buf(2, ty, tx), buf(5, ext, tx), buf(5, ext, tx),
         buf(3 * tx, 2 * tx, dtype=BF16), buf(6 * tx, 2 * tx, dtype=BF16),
-        buf(PACK * ext, 3 * tx, dtype=BF16), buf(levels, ext, tx),
+        buf(PACK * ext, 3 * tx, dtype=BF16), buf(PACK, 2, ext + 16, tx), buf(levels, ext, tx),
         buf(groups + 2, ty, tx), buf(four, ty, tx), buf(two, ty, tx),
         buf(rows, EDGE, tx), buf(rows, EDGE, tx),
         buf(four, ty, tx), buf(two, ty, tx), buf(groups + 2, ty, tx), buf(groups + 2, ty, tx),

time: 31.7 us -> 31.9 us (level)
  no operation moved by 1% of the time
where the time goes in v4:
time: 31.9 us; the launch traced here: 31.6 us
  Pallas kernels  28.6 us (90%)
  local copies, waits for them, and re-layouts  1.68 us (5%)
  between operations  1.29 us (4%)
    pallas_call x1, Pallas kernels, on_device(): pl.pallas_call(functools.partial(kernel, levels), out_shape=(jax.ShapeDty...  28.6 us
    unnamed x2, local copies, waits for them, and re-layouts  1.68 us

profile of v4, /device:TPU:1, one launch (start us, length us, event | category | flops | bytes accessed | tf_op | source)
XLA Modules:
  0.0 31.6 jit_solution(14441085801958702441)
XLA Ops:
  1.3 28.6 %shard_map.104 = (f32[80,32,128]{2,1,0:T(8,128)S(1)}, f32[1,80,128]{2,1,0:T(8,128)S(1)}) custom-call(f32[80,32,128]{2,1,0:T(8,128)} %control_in.1, f32[32,128]{1,0:T(8,128)} %diffusivity_in.1, s32[32,128]{1,0:T(8,128)} %land_mask_in.1, f32[1,80,128]{2,1,0:T(8,128)} %innovations_in.1, f32[1,80,128]{2,1,0:T(8,128)} %sigma_in.1, s32[1,128]{1,0:T(1,128)} %obs_row_in.1, ...), custom_call_target="tpu_custom_call" | custom-call | tf_op jit(solution)/shard_map/pallas_call | solution.py:470
  29.9 1.1 %copy.14 = f32[80,32,128]{2,1,0:T(8,128)} copy(f32[80,32,128]{2,1,0:T(8,128)S(1)} %get-tuple-element.4) | data formatting | bytes 2621440
  31.0 0.6 %copy.15 = f32[1,80,128]{2,1,0:T(8,128)} copy(f32[1,80,128]{2,1,0:T(8,128)S(1)} %get-tuple-element.5) | data formatting | bytes 81920

commit v5 on v3

--- a/solution.py
+++ b/solution.py
@@ -24,8 +24,8 @@
     coeff, weights, strip_weights, hot_in, hot_out, work, adjoint,
     pack, send_e, send_w, rows_up, rows_dn,
     from_w, from_e, pack_e, pack_w, got_up, got_dn, pgot_up, pgot_dn,
-    bpack, brow_up, brow_dn,
-    bpack_e, bpack_w, bgot_up, bgot_dn, bpgot_up, bpgot_dn,
+    bpack, bsend_e, bsend_w, brow_up, brow_dn,
+    bfrom_e, bfrom_w, bpack_e, bpack_w, bgot_up, bgot_dn, bpgot_up, bpgot_dn,
     send_sem, recv_sem, bsend_sem, brecv_sem,
 ):
     ty, tx = control.shape[1], control.shape[2]
@@ -289,21 +289,28 @@
     def dot(x, y, dims, precision=None):
         return lax.dot_general(x, y, (dims, ((), ())), precision=precision, preferred_element_type=F32)
 
-    def back_sides(g):
+    cut = (groups + 1) // 2
+    chunks = ((0, cut), (cut, groups))
+
+    def back_sides(c):
+        lo, hi = chunks[c]
+        e, w = pl.ds(0, -(-(hi - lo) // 2)), pl.ds(0, -(-(hi - lo) // 4))
         return (
-            copy(bpack.at[g], bpack_w.at[g], bsend_sem, brecv_sem, g * 8, east, lat),
-            copy(bpack.at[g], bpack_e.at[g], bsend_sem, brecv_sem, g * 8 + 1, west, lat),
+            copy(bsend_e.at[c, e], bfrom_w.at[c, e], bsend_sem, brecv_sem, c * 8, east, lat),
+            copy(bsend_w.at[c, w], bfrom_e.at[c, w], bsend_sem, brecv_sem, c * 8 + 1, west, lat),
         )
 
-    def back_up(g):
-        return [copy(brow_up.at[g], bgot_dn.at[g], bsend_sem, brecv_sem, g * 8 + 2, lon, lat + 1)] + [
-            copy(brow_up.at[g, PACK], bpgot_dn.at[place[i] - 1, g], bsend_sem, brecv_sem, g * 8 + 3 + i, columns[i], lat + 1)
+    def back_up(c):
+        some = pl.ds(chunks[c][0], chunks[c][1] - chunks[c][0])
+        return [copy(brow_up.at[some], bgot_dn.at[some], bsend_sem, brecv_sem, c * 8 + 2, lon, lat + 1)] + [
+            copy(brow_up.at[some, PACK], bpgot_dn.at[place[i] - 1, some], bsend_sem, brecv_sem, c * 8 + 3 + i, columns[i], lat + 1)
             for i in (1, 2)
         ]
 
-    def back_dn(g):
-        return [copy(brow_dn.at[g], bgot_up.at[g], bsend_sem, brecv_sem, g * 8 + 3, lon, lat - 1)] + [
-            copy(brow_dn.at[g, PACK], bpgot_up.at[place[i] - 1, g], bsend_sem, brecv_sem, g * 8 + 5 + i, columns[i], lat - 1)
+    def back_dn(c):
+        some = pl.ds(chunks[c][0], chunks[c][1] - chunks[c][0])
+        return [copy(brow_dn.at[some], bgot_up.at[some], bsend_sem, brecv_sem, c * 8 + 3, lon, lat - 1)] + [
+            copy(brow_dn.at[some, PACK], bpgot_up.at[place[i] - 1, some], bsend_sem, brecv_sem, c * 8 + 5 + i, columns[i], lat - 1)
             for i in (1, 2)
         ]
 
@@ -346,22 +353,36 @@
         brow_dn[g, 0:PACK] = adjoint[mine, 0:EDGE, :]
         brow_up[g, PACK] = bpack[g, ty - 3 : ty + 1, :]
         brow_dn[g, PACK] = bpack[g, 0:EDGE, :]
-        for c in back_sides(g):
-            c.start()
+        return carry
+
+    def send_back(c):
+        lo, hi = chunks[c]
+        for q in range(-(-(hi - lo) // 2)):
+            acc = bpack[lo + 2 * q]
+            if lo + 2 * q + 1 < hi:
+                acc = jnp.where(slot < 4, acc, pltpu.roll(bpack[lo + 2 * q + 1], 4, 1))
+            bsend_e[c, q] = acc
+        for q in range(-(-(hi - lo) // 4)):
+            acc = pltpu.roll(bpack[lo + 4 * q], tx - 5, 1)
+            for j in range(1, min(4, hi - lo - 4 * q)):
+                acc = jnp.where(slot // 2 == j, pltpu.roll(bpack[lo + 4 * q + j], tx - 5 + 2 * j, 1), acc)
+            bsend_w[c, q] = acc
+        for d in back_sides(c):
+            d.start()
 
         @pl.when(has_up)
         def _():
-            for c in back_up(g):
-                c.start()
+            for d in back_up(c):
+                d.start()
 
         @pl.when(has_dn)
         def _():
-            for c in back_dn(g):
-                c.start()
-
-        return carry
-
-    lax.fori_loop(0, groups, forward, 0)
+            for d in back_dn(c):
+                d.start()
+
+    for c, (lo, hi) in enumerate(chunks):
+        lax.fori_loop(lo, hi, forward, 0)
+        send_back(c)
 
     @pl.when(jnp.logical_not(has_up))
     def _():
@@ -380,29 +401,38 @@
         last = x[ty:ext] + jnp.where(sub8 > 4, low, jnp.concatenate([above, zero], axis=0))
         return jnp.concatenate([first, x[8:ty], last], axis=0)
 
-    def backward(g, carry):
-        for c in back_sides(g):
-            c.wait()
+    def take_back(c):
+        for d in back_sides(c):
+            d.wait()
 
         @pl.when(has_up)
         def _():
-            for c in back_up(g):
-                c.wait_send()
-            for c in back_dn(g):
-                c.wait_recv()
+            for d in back_up(c):
+                d.wait_send()
+            for d in back_dn(c):
+                d.wait_recv()
 
         @pl.when(has_dn)
         def _():
-            for c in back_dn(g):
-                c.wait_send()
-            for c in back_up(g):
-                c.wait_recv()
-
+            for d in back_dn(c):
+                d.wait_send()
+            for d in back_up(c):
+                d.wait_recv()
+
+        for k in range(chunks[c][0], chunks[c][1]):
+            q, j = divmod(k - chunks[c][0], 2)
+            bpack_w[k] = pltpu.roll(bfrom_w[c, q], 1 if j else 5, 1)
+            q, j = divmod(k - chunks[c][0], 4)
+            bpack_e[k] = pltpu.roll(bfrom_e[c, q], (2 - 2 * j) % tx, 1)
+
+    def side_of(x, k, g, distance):
+        ends = pltpu.roll(jnp.concatenate([bpgot_up[k, g], bpgot_dn[k, g]], axis=0), distance, 1)
+        return with_rows(x, ends[0:EDGE], ends[EDGE : 2 * EDGE])
+
+    def backward(g, carry):
         own = with_rows(bpack[g], bgot_up[g, PACK], bgot_dn[g, PACK])
-        e = with_rows(bpack_e[g], bpgot_up[0, g], bpgot_dn[0, g])
-        w = with_rows(bpack_w[g], bpgot_up[1, g], bpgot_dn[1, g])
-        side_e = pltpu.roll(e, tx - 3, 1)
-        side_w = pltpu.roll(w, 5, 1)
+        side_e = side_of(bpack_e[g], 0, g, tx - 3)
+        side_w = side_of(bpack_w[g], 1, g, 5)
         strip = jnp.where(jnp.logical_or(slot < 3, slot == 7), own, 0.0)
         strip = strip + jnp.where(jnp.logical_or(slot == 2, slot == 3), side_e, 0.0)
         strip = strip + jnp.where(slot > 4, side_w, 0.0)
@@ -419,7 +449,9 @@
             gradient[level] = x[0:ty]
         return carry
 
-    lax.fori_loop(0, groups, backward, 0)
+    for c, (lo, hi) in enumerate(chunks):
+        take_back(c)
+        lax.fori_loop(lo, hi, backward, 0)
 
 
 def on_device(
@@ -435,6 +467,8 @@
 
     four, two = -(-(groups + 2) // 4), -(-(groups + 2) // 2)
     rows = levels + groups + 4
+    half = (groups + 1) // 2
+    most_e, most_w = -(-half // 2), -(-half // 4)
     scratch = [
         buf(levels, ty, tx), buf(ty, tx), buf(ty, tx, dtype=jnp.int32),
         buf(*innovations.shape), buf(*obs_sigma.shape),
@@ -448,13 +482,14 @@
         buf(four, ty, tx), buf(two, ty, tx), buf(groups + 2, ty, tx), buf(groups + 2, ty, tx),
         buf(rows, EDGE, tx), buf(rows, EDGE, tx),
         buf(2, groups + 2, EDGE, tx), buf(2, groups + 2, EDGE, tx),
-        buf(groups, ext, tx),
+        buf(groups, ext, tx), buf(2, most_e, ext, tx), buf(2, most_w, ext, tx),
         buf(groups, PACK + 1, EDGE, tx), buf(groups, PACK + 1, EDGE, tx),
+        buf(2, most_w, ext, tx), buf(2, most_e, ext, tx),
         buf(groups, ext, tx), buf(groups, ext, tx),
         buf(groups, PACK + 1, EDGE, tx), buf(groups, PACK + 1, EDGE, tx),
         buf(2, groups, EDGE, tx), buf(2, groups, EDGE, tx),
         pltpu.SemaphoreType.DMA((8,)), pltpu.SemaphoreType.DMA((8,)),
-        pltpu.SemaphoreType.DMA((8 * groups,)), pltpu.SemaphoreType.DMA((8 * groups,)),
+        pltpu.SemaphoreType.DMA((16,)), pltpu.SemaphoreType.DMA((16,)),
     ]
     return pl.pallas_call(
         functools.partial(kernel, levels),

time: 31.7 us -> 35.3 us (1.11)
  Pallas kernels: 28.5 us -> 32.1 us
    pallas_call x1, Pallas kernels: 28.5 us -> 32.1 us  [on_device(): pl.pallas_call(functools.partial(kernel, levels), out_shape=(jax.ShapeDty...]
where the time goes in v5:
time: 35.3 us; the launch traced here: 35.1 us
  Pallas kernels  32.1 us (91%)
  local copies, waits for them, and re-layouts  1.68 us (5%)
  between operations  1.29 us (4%)
    pallas_call x1, Pallas kernels, on_device(): pl.pallas_call(functools.partial(kernel, levels), out_shape=(jax.ShapeDty...  32.1 us
    unnamed x2, local copies, waits for them, and re-layouts  1.68 us

profile of v5, /device:TPU:1, one launch (start us, length us, event | category | flops | bytes accessed | tf_op | source)
XLA Modules:
  0.0 35.1 jit_solution(2680877208989300830)
XLA Ops:
  1.3 32.1 %shard_map.104 = (f32[80,32,128]{2,1,0:T(8,128)S(1)}, f32[1,80,128]{2,1,0:T(8,128)S(1)}) custom-call(f32[80,32,128]{2,1,0:T(8,128)} %control_in.1, f32[32,128]{1,0:T(8,128)} %diffusivity_in.1, s32[32,128]{1,0:T(8,128)} %land_mask_in.1, f32[1,80,128]{2,1,0:T(8,128)} %innovations_in.1, f32[1,80,128]{2,1,0:T(8,128)} %sigma_in.1, s32[1,128]{1,0:T(1,128)} %obs_row_in.1, ...), custom_call_target="tpu_custom_call" | custom-call | tf_op jit(solution)/shard_map/pallas_call | solution.py:494
  33.4 1.1 %copy.14 = f32[80,32,128]{2,1,0:T(8,128)} copy(f32[80,32,128]{2,1,0:T(8,128)S(1)} %get-tuple-element.4) | data formatting | bytes 2621440
  34.4 0.6 %copy.15 = f32[1,80,128]{2,1,0:T(8,128)} copy(f32[1,80,128]{2,1,0:T(8,128)S(1)} %get-tuple-element.5) | data formatting | bytes 81920

commit v6 on v3

--- a/solution.py
+++ b/solution.py
@@ -105,11 +105,15 @@
 
     def pack_group(g, carry):
         fetch_group(g).wait()
-        acc = jnp.zeros((ty, tx), F32)
-        for p in range(PACK):
-            x = control[g * PACK + p]
-            acc = jnp.where(lane_t // SLOT == p, pltpu.roll(x, SLOT * p + 2, 1), acc)
-        pack[g] = acc
+
+        def some(i, acc):
+            for j in range(4):
+                p = i * 4 + j
+                x = control[g * PACK + p]
+                acc = jnp.where(lane_t // SLOT == p, pltpu.roll(x, SLOT * p + 2, 1), acc)
+            return acc
+
+        pack[g] = lax.fori_loop(0, PACK // 4, some, jnp.zeros((ty, tx), F32))
         return carry
 
     lax.fori_loop(0, groups, pack_group, 0)
@@ -257,7 +261,7 @@
         return left, right, pltpu.roll(x, 1, 0), pltpu.roll(x, ext - 1, 0)
 
     def fill_of(edge, p):
-        return pltpu.roll(edge, (tx - 3 - SLOT * p) % tx, 1)
+        return pltpu.roll(edge, lax.rem(2 * tx - 3 - SLOT * p, tx), 1)
 
     def make_weights(dst, kappa, mask, kappas, masks):
         total = jnp.zeros_like(kappa)
@@ -313,15 +317,21 @@
         strip1 = diffuse(strip0, None, strip_weights)
         edge1 = edge_of(strip1)
         strip2 = diffuse(strip1, None, strip_weights)
-        for p in range(0, PACK, 2):
+
+        def some(i, carry):
             pair = []
-            for q in (p, p + 1):
-                level = g * PACK + q
+            for j in range(2):
+                p = i * 2 + j
+                level = g * PACK + p
                 x = jnp.concatenate([control[level], got_up[level], got_dn[level]], axis=0)
-                x = diffuse(x, fill_of(edge0, q), weights)
-                pair.append(diffuse(x, fill_of(edge1, q), weights))
+                x = diffuse(x, fill_of(edge0, p), weights)
+                pair.append(diffuse(x, fill_of(edge1, p), weights))
+            there = pl.ds(pl.multiple_of(i * (2 * ext), 16), 2 * ext)
             for k, part in enumerate(parts(jnp.concatenate(pair, axis=0))):
-                work[p * ext : (p + 2) * ext, k * tx : (k + 1) * tx] = part
+                work[there, k * tx : (k + 1) * tx] = part
+            return carry
+
+        lax.fori_loop(0, PACK // 2, some, 0)
         picked = dot(work[...], hot_in[...], ((1,), (0,)))
         outer = dot(strip2, beyond, ((0,), (0,)), lax.Precision.HIGHEST)
         outer = jnp.sum(jnp.where(sub8[None] == 2, outer.reshape(PACK, SLOT, tx), 0.0), axis=1)
@@ -409,14 +419,20 @@
         first_col = jnp.where(slot == 7, side_w, 0.0)
         edge0 = edge_of(strip)
         edge1 = edge_of(diffuse(strip, None, strip_weights))
-        for p in range(PACK):
-            level = g * PACK + p
-            x = with_rows(adjoint[level], bgot_up[g, p], bgot_dn[g, p])
-            extra = pltpu.roll(first_col, (tx - 7 - SLOT * p) % tx, 1)
-            x = x + jnp.where(lane == 0, extra, 0.0)
-            x = diffuse(x, fill_of(edge0, p), weights)
-            x = diffuse(x, fill_of(edge1, p), weights)
-            gradient[level] = x[0:ty]
+
+        def some(i, carry):
+            for j in range(2):
+                p = i * 2 + j
+                level = g * PACK + p
+                x = with_rows(adjoint[level], bgot_up[g, p], bgot_dn[g, p])
+                extra = pltpu.roll(first_col, lax.rem(2 * tx - 7 - SLOT * p, tx), 1)
+                x = x + jnp.where(lane == 0, extra, 0.0)
+                x = diffuse(x, fill_of(edge0, p), weights)
+                x = diffuse(x, fill_of(edge1, p), weights)
+                gradient[level] = x[0:ty]
+            return carry
+
+        lax.fori_loop(0, PACK // 2, some, 0)
         return carry
 
     lax.fori_loop(0, groups, backward, 0)

time: 31.7 us -> 41 us (1.29)
  Pallas kernels: 28.5 us -> 37.8 us
    pallas_call x1, Pallas kernels: 28.5 us -> 37.8 us  [on_device(): pl.pallas_call(functools.partial(kernel, levels), out_shape=(jax.ShapeDty...]
where the time goes in v6:
time: 41 us; the launch traced here: 40.7 us
  Pallas kernels  37.8 us (92%)
  local copies, waits for them, and re-layouts  1.68 us (4%)
  between operations  1.29 us (3%)
    pallas_call x1, Pallas kernels, on_device(): pl.pallas_call(functools.partial(kernel, levels), out_shape=(jax.ShapeDty...  37.8 us
    unnamed x2, local copies, waits for them, and re-layouts  1.68 us

profile of v6, /device:TPU:1, one launch (start us, length us, event | category | flops | bytes accessed | tf_op | source)
XLA Modules:
  0.0 40.7 jit_solution(758215199871906513)
XLA Ops:
  1.3 37.8 %shard_map.104 = (f32[80,32,128]{2,1,0:T(8,128)S(1)}, f32[1,80,128]{2,1,0:T(8,128)S(1)}) custom-call(f32[80,32,128]{2,1,0:T(8,128)} %control_in.1, f32[32,128]{1,0:T(8,128)} %diffusivity_in.1, s32[32,128]{1,0:T(8,128)} %land_mask_in.1, f32[1,80,128]{2,1,0:T(8,128)} %innovations_in.1, f32[1,80,128]{2,1,0:T(8,128)} %sigma_in.1, s32[1,128]{1,0:T(1,128)} %obs_row_in.1, ...), custom_call_target="tpu_custom_call" | custom-call | tf_op jit(solution)/shard_map/pallas_call | solution.py:475
  39.0 1.1 %copy.14 = f32[80,32,128]{2,1,0:T(8,128)} copy(f32[80,32,128]{2,1,0:T(8,128)S(1)} %get-tuple-element.4) | data formatting | bytes 2621440
  40.1 0.6 %copy.15 = f32[1,80,128]{2,1,0:T(8,128)} copy(f32[1,80,128]{2,1,0:T(8,128)S(1)} %get-tuple-element.5) | data formatting | bytes 81920

commit v7 on v3

--- a/solution.py
+++ b/solution.py
@@ -382,19 +382,15 @@
 
     def backward(g, carry):
         for c in back_sides(g):
-            c.wait()
+            c.wait_recv()
 
         @pl.when(has_up)
         def _():
-            for c in back_up(g):
-                c.wait_send()
             for c in back_dn(g):
                 c.wait_recv()
 
         @pl.when(has_dn)
         def _():
-            for c in back_dn(g):
-                c.wait_send()
             for c in back_up(g):
                 c.wait_recv()
 
@@ -420,6 +416,24 @@
         return carry
 
     lax.fori_loop(0, groups, backward, 0)
+
+    def sent(g, carry):
+        for c in back_sides(g):
+            c.wait_send()
+
+        @pl.when(has_up)
+        def _():
+            for c in back_up(g):
+                c.wait_send()
+
+        @pl.when(has_dn)
+        def _():
+            for c in back_dn(g):
+                c.wait_send()
+
+        return carry
+
+    lax.fori_loop(0, groups, sent, 0)
 
 
 def on_device(

time: 31.7 us -> 31.7 us (level)
  no operation moved by 1% of the time
where the time goes in v7:
time: 31.7 us; the launch traced here: 31.4 us
  Pallas kernels  28.5 us (90%)
  local copies, waits for them, and re-layouts  1.68 us (5%)
  between operations  1.29 us (4%)
    pallas_call x1, Pallas kernels, on_device(): pl.pallas_call(functools.partial(kernel, levels), out_shape=(jax.ShapeDty...  28.5 us
    unnamed x2, local copies, waits for them, and re-layouts  1.68 us

profile of v7, /device:TPU:1, one launch (start us, length us, event | category | flops | bytes accessed | tf_op | source)
XLA Modules:
  0.0 31.4 jit_solution(14971849885311588347)
XLA Ops:
  1.3 28.5 %shard_map.104 = (f32[80,32,128]{2,1,0:T(8,128)S(1)}, f32[1,80,128]{2,1,0:T(8,128)S(1)}) custom-call(f32[80,32,128]{2,1,0:T(8,128)} %control_in.1, f32[32,128]{1,0:T(8,128)} %diffusivity_in.1, s32[32,128]{1,0:T(8,128)} %land_mask_in.1, f32[1,80,128]{2,1,0:T(8,128)} %innovations_in.1, f32[1,80,128]{2,1,0:T(8,128)} %sigma_in.1, s32[1,128]{1,0:T(1,128)} %obs_row_in.1, ...), custom_call_target="tpu_custom_call" | custom-call | tf_op jit(solution)/shard_map/pallas_call | solution.py:473
  29.8 1.1 %copy.14 = f32[80,32,128]{2,1,0:T(8,128)} copy(f32[80,32,128]{2,1,0:T(8,128)S(1)} %get-tuple-element.4) | data formatting | bytes 2621440
  30.8 0.6 %copy.15 = f32[1,80,128]{2,1,0:T(8,128)} copy(f32[1,80,128]{2,1,0:T(8,128)S(1)} %get-tuple-element.5) | data formatting | bytes 81920
